TPU v7x, 512 devices: a whole 4x8x8 slice. The times are simulated.
512 devices in a mesh: leaf: 128 (over z, y, core), sub: 4 (over x).
Axes of the slice: x: 4, y: 8, z: 8, core: 2. Of those that a mesh axis runs over, the one named last changes fastest.
Arguments:
- light: bfloat16 [32, 1048576], P(None, ('leaf', 'sub')), may hold values from -6 to 6
- probes: bfloat16 [4, 1048576], P(None, ('leaf', 'sub')), may hold values from 0 to 1, as said below
- near_list: int32 [4096, 4], P(('leaf', 'sub')), may hold values from 0 to 4095, as said below
- far_list: int32 [4096, 32], P(('leaf', 'sub')), may hold values from 0 to 4095, as said below
- leaf_basis: bfloat16 [4096, 256, 64], P(('leaf', 'sub')), may hold values from -0.375 to 0.375
- leaf_transfer: bfloat16 [4096, 64, 64], P(('leaf', 'sub')), may hold values from -0.25 to 0.25
- far_coupling: bfloat16 [4096, 32, 64, 64], P(('leaf', 'sub')), may hold values from -0.125 to 0.125
- up_transfer: bfloat16 [3, 2, 64, 64], replicated, may hold values from -0.5 to 0.5
- upper_coupling: bfloat16 [4, 2, 64, 64], replicated, may hold values from -0.5 to 0.5
Outputs:
- irradiance: bfloat16 [32, 1048576], P(None, ('leaf', 'sub'))
Inputs may be any that keep to these rules, and one draw needn't show every extreme that they name: `near_list`: each leaf's list names 4 distinct leaves other than itself, each within 4 leaf numbers of it. `far_list`: every entry names a leaf on a device with the same sub index as the leaf's own device and another leaf index. The entries of one device's leaves name leaves of any one other device at most 4 times, and exactly 4 times for some device. `probes`: rows 0 to 2 lie in the unit box, row 3 is positive.
All inputs are finite; a program needn't handle non-finite values.
Results may differ from a plain program's by a relative error of at most 0.0049.
The roundings to bfloat16 on the way count: a program that leaves them out, or rounds other values in their place, can miss the bound.
Values may be sent and summed in bfloat16 or wider, within the bound.
A program may use at most 128 MiB of HBM per device.

v0:
```python
import jax
import jax.numpy as jnp
from jax import lax
from jax.sharding import PartitionSpec as P

HALO = 4
UPLV = 3


soften = 0.0025
spacing = 0.25


def extended(value, sides, width):
    for axis, dim in sides:
        size, length = (lax.axis_size(axis), value.shape[dim])
        up = [(i, (i + 1) % size) for i in range(size - 1)]
        down = [(j, i) for i, j in up]
        last = lax.slice_in_dim(value, length - width, length, axis=dim)
        leading = lax.slice_in_dim(value, 0, width, axis=dim)
        before = lax.ppermute(last, axis, up)
        after = lax.ppermute(leading, axis, down)
        value = jnp.concatenate([before, value, after], axis=dim)
    return value


def from_partner(value, axis, distance):
    mask = 2**distance
    pairs = [(source, source ^ mask) for source in range(lax.axis_size(axis))]
    return lax.ppermute(value, axis, pairs)


def passed_along(value, axis, steps):
    count = lax.axis_size(axis)
    leading, last = (max(0, -steps), min(count, count - steps))
    return lax.ppermute(value, axis, [(source, source + steps) for source in range(leading, last)])


def kernel_block(target_geo, source_geo, offset):
    delta_x = target_geo[0][:, None] - source_geo[0][None, :] + spacing * offset
    delta_y = target_geo[1][:, None] - source_geo[1][None, :]
    delta_z = target_geo[2][:, None] - source_geo[2][None, :]
    square = delta_x * delta_x + delta_y * delta_y + delta_z * delta_z
    return target_geo[3][:, None] * source_geo[3][None, :] * (soften / (soften + square))


def high_product(left_matrix, right_matrix):
    return jnp.dot(left_matrix, right_matrix.astype(jnp.float32), precision=lax.Precision.HIGHEST)


def high_transposed(left_matrix, right_matrix):
    return lax.dot_general(
        left_matrix,
        right_matrix.astype(jnp.float32),
        (((1,), (1,)), ((), ())),
        precision=lax.Precision.HIGHEST,
    )


def per_device(
    light,
    probes,
    near_list,
    far_list,
    leaf_basis,
    leaf_transfer,
    far_coupling,
    up_transfer,
    upper_coupling,
):
    leaf_count = leaf_basis.shape[0]
    leaf_size = leaf_basis.shape[1]
    rank_size = leaf_basis.shape[2]
    light_rows = light.shape[0]
    device_index = lax.axis_index(("leaf", "sub"))
    anchor = device_index * leaf_count
    stacked = jnp.concatenate([light, probes], axis=0)
    padded = extended(stacked, ((("leaf", "sub"), 1),), HALO * leaf_size)
    local_ids = anchor + jnp.arange(leaf_count, dtype=jnp.int32)
    target_geo = probes.astype(jnp.float32).reshape(4, leaf_count, leaf_size)
    tile_maker = jax.vmap(kernel_block, in_axes=(1, 1, None))
    near_terms = jnp.zeros((light_rows, leaf_count, leaf_size), jnp.float32)
    for step in range(-HALO, HALO + 1):
        start = (HALO + step) * leaf_size
        window = padded[:, start : start + leaf_count * leaf_size]
        source_values = window[:light_rows].reshape(light_rows, leaf_count, leaf_size)
        source_geo = window[light_rows:].astype(jnp.float32).reshape(4, leaf_count, leaf_size)
        kernel_tiles = tile_maker(target_geo, source_geo, jnp.float32(-step)).astype(jnp.bfloat16)
        contribution = jnp.einsum(
            "rjl,jil->rji", source_values, kernel_tiles, preferred_element_type=jnp.float32
        )
        if step == 0:
            near_terms = near_terms + contribution
        else:
            chosen = jnp.any(near_list == (local_ids + step)[:, None], axis=1).astype(jnp.float32)
            near_terms = near_terms + contribution * chosen[None, :, None]
    light_blocks = light.reshape(light_rows, leaf_count, leaf_size)
    coefficients = jnp.einsum(
        "rjl,jlk->jrk", light_blocks, leaf_basis, preferred_element_type=jnp.float32
    ).astype(jnp.bfloat16)
    coeff_flat = coefficients.reshape(leaf_count, light_rows * rank_size)
    entries = far_list.reshape(-1)
    groups = lax.axis_size("sub")
    peer_row = entries // leaf_count // groups
    which_leaf = entries % leaf_count
    pooled = lax.all_gather(coeff_flat, "leaf", axis=0, tiled=True)
    picked = pooled[peer_row * leaf_count + which_leaf]
    picked = picked.reshape(leaf_count, -1, light_rows, rank_size)
    far_terms = jnp.einsum(
        "jcrk,jckm->jrm", picked, far_coupling, preferred_element_type=jnp.float32
    )
    upward = [
        jnp.einsum("jrk,jkm->rm", coefficients, leaf_transfer, preferred_element_type=jnp.float32)
    ]
    for height in range(UPLV):
        parity = device_index >> height & 1
        mine_term = high_product(upward[-1], up_transfer[height][parity])
        other_term = from_partner(mine_term, ("leaf", "sub"), height)
        left_term = jnp.where(parity == 0, mine_term, other_term)
        right_term = jnp.where(parity == 0, other_term, mine_term)
        upward.append(left_term + right_term)
    downward = None
    for height in range(UPLV, -1, -1):
        stride = 2 ** (height + 1)
        lower_part = passed_along(upward[height], ("leaf", "sub"), stride)
        upper_part = passed_along(upward[height], ("leaf", "sub"), -stride)
        coupled = high_product(lower_part, upper_coupling[height, 0]) + high_product(
            upper_part, upper_coupling[height, 1]
        )
        if downward is not None:
            parity = device_index >> height & 1
            coupled = coupled + high_transposed(downward, up_transfer[height][parity])
        downward = coupled
    pulled = jnp.einsum(
        "rk,jmk->jrm", downward, leaf_transfer.astype(jnp.float32), precision=lax.Precision.HIGHEST
    )
    leaf_far = (far_terms + pulled).astype(jnp.bfloat16)
    spread = jnp.einsum("jrk,jlk->rjl", leaf_far, leaf_basis, preferred_element_type=jnp.float32)
    combined = near_terms + spread
    return combined.reshape(light_rows, leaf_count * leaf_size).astype(jnp.bfloat16)


def solution(mesh):
    return jax.shard_map(
        per_device,
        mesh=mesh,
        in_specs=(
            P(None, ("leaf", "sub")),
            P(None, ("leaf", "sub")),
            P(("leaf", "sub"), None),
            P(("leaf", "sub"), None),
            P(("leaf", "sub"), None, None),
            P(("leaf", "sub"), None, None),
            P(("leaf", "sub"), None, None, None),
            P(),
            P(),
        ),
        out_specs=P(None, ("leaf", "sub")),
        check_vma=False,
    )
```

profile of v0, /device:TPU:1, one launch (start us, length us, event | category | flops | bytes accessed | tf_op | source)
XLA Modules:
  0.0 131.3 jit_solution(11800955980936551876)
XLA Ops:
  6.5 0.9 copy-done
  7.5 1.1 convolution_convert_fusion
  8.6 1.1 convolution_bitcast_fusion.3
  9.7 6.0 %collective-permute-start.3 = (f32[32,64]{1,0:T(8,128)S(1)}, f32[32,64]{1,0:T(8,128)S(1)}, u32[]{:S(2)}, u32[]{:S(2)}) collective-permute-start(f32[32,64]{1,0:T(8,128)S(1)} %convolution_bitcast_fusion.3), channel_id=1, source_target_pairs={{2,0},{3,1},{4,2},{5,3},{6,4},{7,5},{8,6},{9,7},{10,8},{11,9},{12,... | collective-permute-start | bytes 24584 | tf_op jit(solution)/shard_map/ppermute | solution.py:36
  15.7 1.9 %collective-permute-start.2 = (f32[32,64]{1,0:T(8,128)S(1)}, f32[32,64]{1,0:T(8,128)S(1)}, u32[]{:S(2)}, u32[]{:S(2)}) collective-permute-start(f32[32,64]{1,0:T(8,128)S(1)} %convolution_bitcast_fusion.3), channel_id=1, source_target_pairs={{0,2},{1,3},{2,4},{3,5},{4,6},{5,7},{6,8},{7,9},{8,10},{9,11},{10,... | collective-permute-start | bytes 24584 | tf_op jit(solution)/shard_map/ppermute | solution.py:36
  17.7 0.8 fusion.206
  18.5 0.1 fusion.154
  18.6 2.8 %collective-permute-start.4 = (f32[32,64]{1,0:T(8,128)S(1)}, f32[32,64]{1,0:T(8,128)S(1)}, u32[]{:S(2)}, u32[]{:S(2)}) collective-permute-start(f32[32,64]{1,0:T(8,128)S(1)} %fusion.154), channel_id=1, source_target_pairs={{0,1},{1,0},{2,3},{3,2},{4,5},{5,4},{6,7},{7,6},{8,9},{9,8},{10,11... | collective-permute-start | bytes 24584 | tf_op jit(solution)/shard_map/ppermute | solution.py:30
  21.4 0.7 reshape.385
  22.2 0.9 constant_dynamic-update-slice_fusion.1
  23.1 0.8 fusion.207
  23.9 2.5 %collective-permute-start = (bf16[36,1024]{1,0:T(8,128)(2,1)S(1)}, bf16[36,1024]{1,0:T(8,128)(2,1)S(1)}, u32[]{:S(2)}, u32[]{:S(2)}) collective-permute-start(bf16[36,1024]{1,0:T(8,128)(2,1)S(1)} %get-tuple-element.74), channel_id=1, source_target_pairs={{0,1},{1,2},{2,3},{3,4},{4,5},{5,6},{6,7},{7,8},{8,9},{9,10},{10,1... | collective-permute-start | bytes 221192 | tf_op jit(solution)/shard_map/ppermute | solution.py:21
  26.4 6.9 %collective-permute-start.1 = (bf16[36,1024]{1,0:T(8,128)(2,1)S(1)}, bf16[36,1024]{1,0:T(8,128)(2,1)S(1)}, u32[]{:S(2)}, u32[]{:S(2)}) collective-permute-start(bf16[36,1024]{1,0:T(8,128)(2,1)S(1)} %get-tuple-element.73), channel_id=1, source_target_pairs={{1,0},{2,1},{3,2},{4,3},{5,4},{6,5},{7,6},{8,7},{9,8},{10,9},{11,1... | collective-permute-start | bytes 221192 | tf_op jit(solution)/shard_map/ppermute | solution.py:22
  33.4 0.8 reshape.386
  34.2 0.1 slice_reduce_fusion.35
  34.3 0.7 compare_reduce_fusion
  35.2 3.1 %collective-permute-start.6 = (f32[32,64]{1,0:T(8,128)S(1)}, f32[32,64]{1,0:T(8,128)S(1)}, u32[]{:S(2)}, u32[]{:S(2)}) collective-permute-start(f32[32,64]{1,0:T(8,128)S(1)} %select_add_fusion.2), channel_id=1, source_target_pairs={{4,0},{5,1},{6,2},{7,3},{8,4},{9,5},{10,6},{11,7},{12,8},{13,9},{1... | collective-permute-start | bytes 24584 | tf_op jit(solution)/shard_map/ppermute | solution.py:36
  38.3 0.1 fusion.147
  38.5 4.3 %collective-permute-start.7 = (f32[32,64]{1,0:T(8,128)S(1)}, f32[32,64]{1,0:T(8,128)S(1)}, u32[]{:S(2)}, u32[]{:S(2)}) collective-permute-start(f32[32,64]{1,0:T(8,128)S(1)} %fusion.147), channel_id=1, source_target_pairs={{0,2},{1,3},{2,0},{3,1},{4,6},{5,7},{6,4},{7,5},{8,10},{9,11},{10,... | collective-permute-start | bytes 24584 | tf_op jit(solution)/shard_map/ppermute | solution.py:30
  42.8 0.1 fusion.156
  42.9 1.7 %collective-permute-done.7 = f32[32,64]{1,0:T(8,128)S(1)} collective-permute-done((f32[32,64]{1,0:T(8,128)S(1)}, f32[32,64]{1,0:T(8,128)S(1)}, u32[]{:S(2)}, u32[]{:S(2)}) %collective-permute-start.7) | collective-permute-done | bytes 8224 | tf_op jit(solution)/shard_map/ppermute | solution.py:30
  44.6 3.4 %collective-permute-start.5 = (f32[32,64]{1,0:T(8,128)S(1)}, f32[32,64]{1,0:T(8,128)S(1)}, u32[]{:S(2)}, u32[]{:S(2)}) collective-permute-start(f32[32,64]{1,0:T(8,128)S(1)} %select_add_fusion.2), channel_id=1, source_target_pairs={{0,4},{1,5},{2,6},{3,7},{4,8},{5,9},{6,10},{7,11},{8,12},{9,13},{1... | collective-permute-start | bytes 24584 | tf_op jit(solution)/shard_map/ppermute | solution.py:36
  48.0 0.1 fusion.140
  48.2 1.9 %collective-permute-start.10 = (f32[32,64]{1,0:T(8,128)S(1)}, f32[32,64]{1,0:T(8,128)S(1)}, u32[]{:S(2)}, u32[]{:S(2)}) collective-permute-start(f32[32,64]{1,0:T(8,128)S(1)} %fusion.140), channel_id=1, source_target_pairs={{0,4},{1,5},{2,6},{3,7},{4,0},{5,1},{6,2},{7,3},{8,12},{9,13},{10,... | collective-permute-start | bytes 24584 | tf_op jit(solution)/shard_map/ppermute | solution.py:30
  50.1 0.1 fusion.149
  50.2 1.0 collective-permute-done.10
  51.3 1.3 collective-permute-start.9
  52.6 3.6 %collective-permute-done.9 = f32[32,64]{1,0:T(8,128)S(1)} collective-permute-done((f32[32,64]{1,0:T(8,128)S(1)}, f32[32,64]{1,0:T(8,128)S(1)}, u32[]{:S(2)}, u32[]{:S(2)}) %collective-permute-start.9) | collective-permute-done | bytes 8224 | tf_op jit(solution)/shard_map/ppermute | solution.py:36
  56.2 1.3 collective-permute-start.12
  57.4 0.1 fusion.142
  57.6 5.8 %collective-permute-done.12 = f32[32,64]{1,0:T(8,128)S(1)} collective-permute-done((f32[32,64]{1,0:T(8,128)S(1)}, f32[32,64]{1,0:T(8,128)S(1)}, u32[]{:S(2)}, u32[]{:S(2)}) %collective-permute-start.12) | collective-permute-done | bytes 8224 | tf_op jit(solution)/shard_map/ppermute | solution.py:36
  63.4 5.1 %collective-permute-start.11 = (f32[32,64]{1,0:T(8,128)S(1)}, f32[32,64]{1,0:T(8,128)S(1)}, u32[]{:S(2)}, u32[]{:S(2)}) collective-permute-start(f32[32,64]{1,0:T(8,128)S(1)} %select_add_fusion), channel_id=1, source_target_pairs={{0,16},{1,17},{2,18},{3,19},{4,20},{5,21},{6,22},{7,23},{8,24},{9,... | collective-permute-start | bytes 24584 | tf_op jit(solution)/shard_map/ppermute | solution.py:36
  68.4 0.1 fusion.135
  68.5 0.7 collective-permute-done.11
  69.3 4.5 %collective-permute-start.8 = (f32[32,64]{1,0:T(8,128)S(1)}, f32[32,64]{1,0:T(8,128)S(1)}, u32[]{:S(2)}, u32[]{:S(2)}) collective-permute-start(f32[32,64]{1,0:T(8,128)S(1)} %select_add_fusion.1), channel_id=1, source_target_pairs={{0,8},{1,9},{2,10},{3,11},{4,12},{5,13},{6,14},{7,15},{8,16},{9,17... | collective-permute-start | bytes 24584 | tf_op jit(solution)/shard_map/ppermute | solution.py:36
  73.8 0.1 convolution_add_fusion.1
  73.9 0.1 fusion.138
  74.0 0.6 collective-permute-done.8
  74.6 0.1 fusion.13
  74.8 0.1 fusion.145
  74.9 0.1 fusion.14
  75.1 0.1 fusion.152
  75.2 0.1 fusion.16
  75.5 0.2 slice_reduce_fusion.27
  75.7 0.2 slice_reduce_fusion.19
  76.0 0.2 slice_reduce_fusion.11
  76.3 0.2 slice_reduce_fusion.3
  76.5 0.1 pad_maximum_fusion
  76.6 2.7 %convolution_multiply_fusion.7 = f32[8,256,32]{1,2,0:T(8,128)S(1)} fusion(f32[8,256]{1,0:T(8,128)S(1)} %sub.188, f32[8,256]{1,0:T(8,128)S(1)} %sub.186, f32[8,256]{1,0:T(8,128)S(1)} %sub.183, f32[8,256]{1,0:T(8,128)S(1)} %sub.181, f32[8,256]{1,0:T(8,128)S(1)} %sub.178, f32[8,256]{1,0:T(8,128)S(1)} %sub.176, f32[8,256]{1,0:T(8,128)S(1)} %mul.326, ...), kind=kOutput, calls=%fused_computation.28 | convolution fusion | flops 40960000 | bytes 458784 | tf_op jit(solution)/shard_map/rjl,jil->rji/dot_general | solution.py:89
  79.3 2.6 %fusion.8 = f32[8,256,32]{1,2,0:T(8,128)S(1)} fusion(f32[8,256,32]{1,2,0:T(8,128)S(1)} %convolution_multiply_fusion.7, f32[8,256]{1,0:T(8,128)S(1)} %sub.388, f32[8,256]{1,0:T(8,128)S(1)} %sub.385, f32[8,256]{1,0:T(8,128)S(1)} %sub.382, f32[8,256]{1,0:T(8,128)S(1)} %mul.337, f32[8,256]{1,0:T(8,128)S(1)} %sub.186, f32[8,256]{1,0:T(8,128)S(1)} %sub.181, ...), kind=kOutput, calls=%fused_computation.27 | convolution fusion | flops 41025536 | bytes 720928 | tf_op jit(solution)/shard_map/rjl,jil->rji/dot_general | solution.py:89
  81.9 2.7 %fusion.7 = f32[8,256,32]{1,2,0:T(8,128)S(1)} fusion(f32[8,256,32]{1,2,0:T(8,128)S(1)} %fusion.8, f32[8,256]{1,0:T(8,128)S(1)} %sub.397, f32[8,256]{1,0:T(8,128)S(1)} %sub.394, f32[8,256]{1,0:T(8,128)S(1)} %sub.391, f32[8,256]{1,0:T(8,128)S(1)} %mul.346, f32[8,256]{1,0:T(8,128)S(1)} %sub.186, f32[8,256]{1,0:T(8,128)S(1)} %sub.181, f32[8,256]{1,0:T(8,128)S(1)} %sub.176, ...), kind=kOutput, calls=%fused_computation.25 | convolution fusion | flops 41025536 | bytes 720928 | tf_op jit(solution)/shard_map/rjl,jil->rji/dot_general | solution.py:89
  84.6 2.6 %fusion.6 = f32[8,256,32]{1,2,0:T(8,128)S(1)} fusion(f32[8,256,32]{1,2,0:T(8,128)S(1)} %fusion.7, f32[8,256]{1,0:T(8,128)S(1)} %sub.406, f32[8,256]{1,0:T(8,128)S(1)} %sub.403, f32[8,256]{1,0:T(8,128)S(1)} %sub.400, f32[8,256]{1,0:T(8,128)S(1)} %mul.355, f32[8,256]{1,0:T(8,128)S(1)} %sub.186, f32[8,256]{1,0:T(8,128)S(1)} %sub.181, f32[8,256]{1,0:T(8,128)S(1)} %sub.176, ...), kind=kOutput, calls=%fused_computation.23 | convolution fusion | flops 41025536 | bytes 720928 | tf_op jit(solution)/shard_map/rjl,jil->rji/dot_general | solution.py:89
  87.2 2.6 %convolution_add_fusion = f32[8,256,32]{1,2,0:T(8,128)S(1)} fusion(f32[8,256,32]{1,2,0:T(8,128)S(1)} %fusion.6, f32[8,256]{1,0:T(8,128)S(1)} %sub.186, f32[8,256]{1,0:T(8,128)S(1)} %sub.181, f32[8,256]{1,0:T(8,128)S(1)} %sub.176, f32[8,256]{1,0:T(8,128)S(1)} %mul.324, bf16[4,8,8,256]{3,2,1,0:T(8,128)(2,1)S(1)} %bitcast.128), kind=kOutput, calls=%fused_computation.21 | convolution fusion | flops 40435712 | bytes 688128 | tf_op jit(solution)/shard_map/rjl,jil->rji/dot_general | solution.py:89
  89.9 2.6 %fusion.5 = f32[8,256,32]{1,2,0:T(8,128)S(1)} fusion(f32[8,256,32]{1,2,0:T(8,128)S(1)} %convolution_add_fusion, f32[8,256]{1,0:T(8,128)S(1)} %sub.421, f32[8,256]{1,0:T(8,128)S(1)} %sub.418, f32[8,256]{1,0:T(8,128)S(1)} %sub.415, f32[8,256]{1,0:T(8,128)S(1)} %mul.370, f32[8,256]{1,0:T(8,128)S(1)} %sub.186, f32[8,256]{1,0:T(8,128)S(1)} %sub.181, ...), kind=kOutput, calls=%fused_computation.20 | convolution fusion | flops 41025536 | bytes 720928 | tf_op jit(solution)/shard_map/rjl,jil->rji/dot_general | solution.py:89
  92.5 2.6 %fusion.4 = f32[8,256,32]{1,2,0:T(8,128)S(1)} fusion(f32[8,256,32]{1,2,0:T(8,128)S(1)} %fusion.5, f32[8,256]{1,0:T(8,128)S(1)} %sub.430, f32[8,256]{1,0:T(8,128)S(1)} %sub.427, f32[8,256]{1,0:T(8,128)S(1)} %sub.424, f32[8,256]{1,0:T(8,128)S(1)} %mul.380, f32[8,256]{1,0:T(8,128)S(1)} %sub.186, f32[8,256]{1,0:T(8,128)S(1)} %sub.181, f32[8,256]{1,0:T(8,128)S(1)} %sub.176, ...), kind=kOutput, calls=%fused_computation.18 | convolution fusion | flops 41025536 | bytes 720928 | tf_op jit(solution)/shard_map/rjl,jil->rji/dot_general | solution.py:89
  95.1 2.6 %fusion.3 = f32[8,256,32]{1,2,0:T(8,128)S(1)} fusion(f32[8,256,32]{1,2,0:T(8,128)S(1)} %fusion.4, f32[8,256]{1,0:T(8,128)S(1)} %sub.439, f32[8,256]{1,0:T(8,128)S(1)} %sub.436, f32[8,256]{1,0:T(8,128)S(1)} %sub.433, f32[8,256]{1,0:T(8,128)S(1)} %mul.390, f32[8,256]{1,0:T(8,128)S(1)} %sub.186, f32[8,256]{1,0:T(8,128)S(1)} %sub.181, f32[8,256]{1,0:T(8,128)S(1)} %sub.176, ...), kind=kOutput, calls=%fused_computation.16 | convolution fusion | flops 41025536 | bytes 720928 | tf_op jit(solution)/shard_map/rjl,jil->rji/dot_general | solution.py:89
  97.8 2.7 %fusion.2 = f32[32,8,256]{2,0,1:T(8,128)} fusion(f32[8,256,32]{1,2,0:T(8,128)S(1)} %fusion.3, f32[8,256]{1,0:T(8,128)S(1)} %sub.448, f32[8,256]{1,0:T(8,128)S(1)} %sub.445, f32[8,256]{1,0:T(8,128)S(1)} %sub.442, f32[8,256]{1,0:T(8,128)S(1)} %mul.400, f32[8,256]{1,0:T(8,128)S(1)} %sub.186, f32[8,256]{1,0:T(8,128)S(1)} %sub.181, f32[8,256]{1,0:T(8,128)S(1)} %sub.176, ...), kind=kOutput, calls=%fused_computation.14 | convolution fusion | flops 41025536 | bytes 720928 | tf_op jit(solution)/shard_map/rjl,jil->rji/dot_general | solution.py:89
  100.5 12.3 %all-gather.2.cloned.1.call-done = bf16[1024,2048]{1,0:T(8,128)(2,1)} async-done(((bf16[8,2048]{1,0:T(8,128)(2,1)}), bf16[1024,2048]{1,0:T(8,128)(2,1)}) %all-gather.2.cloned.1.call-update) | async-done | bytes 4194320 | tf_op jit(solution)/shard_map/all_gather | solution.py:106
  112.8 5.1 %gather_fusion = bf16[256,2048]{1,0:T(8,128)(2,1)S(1)} fusion(bf16[1024,2048]{1,0:T(8,128)(2,1)} %all-gather.2.cloned.1.call-done, s32[1024]{0:T(1024)S(1)} %pad_clamp_fusion), kind=kCustom, calls=%fused_computation | custom fusion | bytes 2098176 | tf_op jit(solution)/shard_map/gather | solution.py:107
  117.9 2.2 %reshape.387 = bf16[8,32,32,64]{3,2,1,0:T(8,128)(2,1)S(1)} reshape(bf16[256,2048]{1,0:T(8,128)(2,1)S(1)} %gather_fusion) | data formatting | bytes 2097152 | tf_op jit(solution)/shard_map/reshape | solution.py:108
  120.1 3.0 %convolution_bitcast_fusion.1 = f32[8,32,64]{2,1,0:T(8,128)S(1)} fusion(bf16[8,32,32,64]{3,2,1,0:T(8,128)(2,1)S(1)} %reshape.387, bf16[8,32,64,64]{3,2,1,0:T(8,128)(2,1)} %param.15), kind=kOutput, calls=%fused_computation.31 | convolution fusion | flops 67108864 | bytes 3211264 | tf_op jit(solution)/shard_map/jcrk,jckm->jrm/dot_general | solution.py:109
  123.1 0.5 fusion.12
  123.6 0.2 fusion.10
  123.8 0.7 copy.33
  (73 shorter events, 0.4 us)
Async XLA Ops:
  6.5 1.0 copy-start
  6.5 36.3 %copy-start.4 = (bf16[4,2,64,64]{3,2,1,0:T(8,128)(2,1)S(1)}, bf16[4,2,64,64]{3,2,1,0:T(8,128)(2,1)}, u32[]{:S(2)}) copy-start(bf16[4,2,64,64]{3,2,1,0:T(8,128)(2,1)} %param.17) | copy-start | bytes 196612
  6.5 106.2 %all-gather.2.cloned.1.call-start = ((), (), s32[]{:S(2)}) async-start(), calls=%async_computation | async-start | bytes 4227072 | tf_op jit(solution)/shard_map/all_gather | solution.py:106
  9.7 28.8 %collective-permute-start.3 = (f32[32,64]{1,0:T(8,128)S(1)}, f32[32,64]{1,0:T(8,128)S(1)}, u32[]{:S(2)}, u32[]{:S(2)}) collective-permute-start(f32[32,64]{1,0:T(8,128)S(1)} %convolution_bitcast_fusion.3), channel_id=1, source_target_pairs={{2,0},{3,1},{4,2},{5,3},{6,4},{7,5},{8,6},{9,7},{10,8},{11,9},{12,... | collective-permute-start | bytes 24584 | tf_op jit(solution)/shard_map/ppermute | solution.py:36
  15.7 59.5 %collective-permute-start.2 = (f32[32,64]{1,0:T(8,128)S(1)}, f32[32,64]{1,0:T(8,128)S(1)}, u32[]{:S(2)}, u32[]{:S(2)}) collective-permute-start(f32[32,64]{1,0:T(8,128)S(1)} %convolution_bitcast_fusion.3), channel_id=1, source_target_pairs={{0,2},{1,3},{2,4},{3,5},{4,6},{5,7},{6,8},{7,9},{8,10},{9,11},{10,... | collective-permute-start | bytes 24584 | tf_op jit(solution)/shard_map/ppermute | solution.py:36
  18.6 16.5 %collective-permute-start.4 = (f32[32,64]{1,0:T(8,128)S(1)}, f32[32,64]{1,0:T(8,128)S(1)}, u32[]{:S(2)}, u32[]{:S(2)}) collective-permute-start(f32[32,64]{1,0:T(8,128)S(1)} %fusion.154), channel_id=1, source_target_pairs={{0,1},{1,0},{2,3},{3,2},{4,5},{5,4},{6,7},{7,6},{8,9},{9,8},{10,11... | collective-permute-start | bytes 24584 | tf_op jit(solution)/shard_map/ppermute | solution.py:30
  23.9 51.5 %collective-permute-start = (bf16[36,1024]{1,0:T(8,128)(2,1)S(1)}, bf16[36,1024]{1,0:T(8,128)(2,1)S(1)}, u32[]{:S(2)}, u32[]{:S(2)}) collective-permute-start(bf16[36,1024]{1,0:T(8,128)(2,1)S(1)} %get-tuple-element.74), channel_id=1, source_target_pairs={{0,1},{1,2},{2,3},{3,4},{4,5},{5,6},{6,7},{7,8},{8,9},{9,10},{10,1... | collective-permute-start | bytes 221192 | tf_op jit(solution)/shard_map/ppermute | solution.py:21
  26.4 49.0 %collective-permute-start.1 = (bf16[36,1024]{1,0:T(8,128)(2,1)S(1)}, bf16[36,1024]{1,0:T(8,128)(2,1)S(1)}, u32[]{:S(2)}, u32[]{:S(2)}) collective-permute-start(bf16[36,1024]{1,0:T(8,128)(2,1)S(1)} %get-tuple-element.73), channel_id=1, source_target_pairs={{1,0},{2,1},{3,2},{4,3},{5,4},{6,5},{7,6},{8,7},{9,8},{10,9},{11,1... | collective-permute-start | bytes 221192 | tf_op jit(solution)/shard_map/ppermute | solution.py:22
  35.2 13.0 %collective-permute-start.6 = (f32[32,64]{1,0:T(8,128)S(1)}, f32[32,64]{1,0:T(8,128)S(1)}, u32[]{:S(2)}, u32[]{:S(2)}) collective-permute-start(f32[32,64]{1,0:T(8,128)S(1)} %select_add_fusion.2), channel_id=1, source_target_pairs={{4,0},{5,1},{6,2},{7,3},{8,4},{9,5},{10,6},{11,7},{12,8},{13,9},{1... | collective-permute-start | bytes 24584 | tf_op jit(solution)/shard_map/ppermute | solution.py:36
  38.5 6.1 %collective-permute-start.7 = (f32[32,64]{1,0:T(8,128)S(1)}, f32[32,64]{1,0:T(8,128)S(1)}, u32[]{:S(2)}, u32[]{:S(2)}) collective-permute-start(f32[32,64]{1,0:T(8,128)S(1)} %fusion.147), channel_id=1, source_target_pairs={{0,2},{1,3},{2,0},{3,1},{4,6},{5,7},{6,4},{7,5},{8,10},{9,11},{10,... | collective-permute-start | bytes 24584 | tf_op jit(solution)/shard_map/ppermute | solution.py:30
  44.6 30.3 %collective-permute-start.5 = (f32[32,64]{1,0:T(8,128)S(1)}, f32[32,64]{1,0:T(8,128)S(1)}, u32[]{:S(2)}, u32[]{:S(2)}) collective-permute-start(f32[32,64]{1,0:T(8,128)S(1)} %select_add_fusion.2), channel_id=1, source_target_pairs={{0,4},{1,5},{2,6},{3,7},{4,8},{5,9},{6,10},{7,11},{8,12},{9,13},{1... | collective-permute-start | bytes 24584 | tf_op jit(solution)/shard_map/ppermute | solution.py:36
  48.2 3.1 %collective-permute-start.10 = (f32[32,64]{1,0:T(8,128)S(1)}, f32[32,64]{1,0:T(8,128)S(1)}, u32[]{:S(2)}, u32[]{:S(2)}) collective-permute-start(f32[32,64]{1,0:T(8,128)S(1)} %fusion.140), channel_id=1, source_target_pairs={{0,4},{1,5},{2,6},{3,7},{4,0},{5,1},{6,2},{7,3},{8,12},{9,13},{10,... | collective-permute-start | bytes 24584 | tf_op jit(solution)/shard_map/ppermute | solution.py:30
  51.3 4.9 %collective-permute-start.9 = (f32[32,64]{1,0:T(8,128)S(1)}, f32[32,64]{1,0:T(8,128)S(1)}, u32[]{:S(2)}, u32[]{:S(2)}) collective-permute-start(f32[32,64]{1,0:T(8,128)S(1)} %select_add_fusion.1), channel_id=1, source_target_pairs={{8,0},{9,1},{10,2},{11,3},{12,4},{13,5},{14,6},{15,7},{16,8},{17,9... | collective-permute-start | bytes 24584 | tf_op jit(solution)/shard_map/ppermute | solution.py:36
  56.2 7.2 %collective-permute-start.12 = (f32[32,64]{1,0:T(8,128)S(1)}, f32[32,64]{1,0:T(8,128)S(1)}, u32[]{:S(2)}, u32[]{:S(2)}) collective-permute-start(f32[32,64]{1,0:T(8,128)S(1)} %select_add_fusion), channel_id=1, source_target_pairs={{16,0},{17,1},{18,2},{19,3},{20,4},{21,5},{22,6},{23,7},{24,8},{25... | collective-permute-start | bytes 24584 | tf_op jit(solution)/shard_map/ppermute | solution.py:36
  63.4 5.9 %collective-permute-start.11 = (f32[32,64]{1,0:T(8,128)S(1)}, f32[32,64]{1,0:T(8,128)S(1)}, u32[]{:S(2)}, u32[]{:S(2)}) collective-permute-start(f32[32,64]{1,0:T(8,128)S(1)} %select_add_fusion), channel_id=1, source_target_pairs={{0,16},{1,17},{2,18},{3,19},{4,20},{5,21},{6,22},{7,23},{8,24},{9,... | collective-permute-start | bytes 24584 | tf_op jit(solution)/shard_map/ppermute | solution.py:36
  69.3 5.4 %collective-permute-start.8 = (f32[32,64]{1,0:T(8,128)S(1)}, f32[32,64]{1,0:T(8,128)S(1)}, u32[]{:S(2)}, u32[]{:S(2)}) collective-permute-start(f32[32,64]{1,0:T(8,128)S(1)} %select_add_fusion.1), channel_id=1, source_target_pairs={{0,8},{1,9},{2,10},{3,11},{4,12},{5,13},{6,14},{7,15},{8,16},{9,17... | collective-permute-start | bytes 24584 | tf_op jit(solution)/shard_map/ppermute | solution.py:36
  84.6 2.6 %copy-start.1 = (bf16[32,2048]{1,0:T(8,128)(2,1)S(1)}, bf16[32,2048]{1,0:T(8,128)(2,1)}, u32[]{:S(2)}) copy-start(bf16[32,2048]{1,0:T(8,128)(2,1)} %param.9) | copy-start | bytes 393220
  120.1 3.1 %copy-start.2 = (bf16[8,64,64]{2,1,0:T(8,128)(2,1)S(1)}, bf16[8,64,64]{2,1,0:T(8,128)(2,1)}, u32[]{:S(2)}) copy-start(bf16[8,64,64]{2,1,0:T(8,128)(2,1)} %param.14) | copy-start | bytes 196612
  120.1 3.5 %copy-start.3 = (f32[32,8,256]{2,0,1:T(8,128)S(1)}, f32[32,8,256]{2,0,1:T(8,128)}, u32[]{:S(2)}) copy-start(f32[32,8,256]{2,0,1:T(8,128)} %fusion.2) | copy-start | bytes 786436
Sparse Core Ops, SparseCore 0:
  22.3 90.4 all-gather.1
where the time goes:
time: 132 us; the launch traced here: 131 us
  starting transfers between devices  45.1 us (34%)
  matrix products  31.5 us (24%)
  waiting for transfers between devices  25.8 us (20%)
  between operations  14.2 us (11%)
  local copies, waits for them, and re-layouts  13.1 us (10%)
  other arithmetic  1.75 us (1%)
    ppermute x8, starting transfers between devices, passed_along(): lax.ppermute(value, axis, [(source, source + steps) for source in range(l...  26.6 us
    dot_general x9, matrix products, per_device(): jnp.einsum('rjl,jil->rji', source_values, kernel_tiles, preferred_element...  23.8 us
    all_gather x1, waiting for transfers between devices, per_device(): pooled = lax.all_gather(coeff_flat, 'leaf', axis=0, tiled=True)  12.3 us
    ppermute x8, waiting for transfers between devices, passed_along(): lax.ppermute(value, axis, [(source, source + steps) for source in range(l...  10.8 us
    ppermute x3, starting transfers between devices, from_partner(): return lax.ppermute(value, axis, pairs)  9.02 us
    ppermute x1, starting transfers between devices, extended(): after = lax.ppermute(leading, axis, down)  6.9 us
    gather x1, local copies, waits for them, and re-layouts, per_device(): picked = pooled[peer_row * leaf_count + which_leaf]  5.09 us
    dot_general x1, matrix products, per_device(): jnp.einsum('jcrk,jckm->jrm', picked, far_coupling, preferred_element_type...  3.03 us
  transfers between devices with their start and end apart: 14, of which 7 were waited for; matrix products, arithmetic and copies ran while one was open for 24% of the time, Pallas kernels for 0%

commit v1 on v0

v1 whole, which is shorter than its diff:
```python
import functools

import jax
import jax.numpy as jnp
from jax import lax
from jax.experimental import pallas as pl
from jax.experimental.pallas import tpu as pltpu
from jax.sharding import PartitionSpec as P

MESH = pl.DeviceIdType.MESH
F32, BF16 = jnp.float32, jnp.bfloat16
HIGH = lax.Precision.HIGHEST

HALO = 4
UPLV = 3
LEAF = 256
RANK = 64
LIGHTS = 32
LEAVES = 8
NNEAR = 4
NFAR = 32
soften = 0.0025
spacing = 0.25

RING = 8
LINE = RING * RING
PER_CHIP = 4
STEPS = RING * RING // 2
WHOLE = 16
HALVES = 24

NT = (((1,), (1,)), ((), ()))


def offset_of(j):
    return ((j + 1) // 2) * (1 - 2 * (j % 2))


def kernel(
    devices,
    light_hbm,
    probes_ref,
    near_list_ref,
    far_list_ref,
    basis_hbm,
    transfer_hbm,
    coupling_hbm,
    up_ref,
    upper_ref,
    out_ref,
    window,
    geo,
    columns,
    basis,
    transfer,
    coupling,
    pool,
    traded,
    near_terms,
    pulled,
    tile,
    upward,
    mine,
    partner,
    below,
    above,
    mask,
    load_sem,
    halo_send,
    halo_recv,
    trade_send,
    trade_recv,
    line_send,
    line_recv,
    right_send,
    right_recv,
    left_send,
    left_recv,
    sib_send,
    sib_recv,
    tree_send,
    tree_recv,
):
    leaf = lax.axis_index("leaf")
    sub = lax.axis_index("sub")
    me = leaf * 4 + sub
    core = leaf % 2
    y = (leaf // 2) % RING
    z = leaf // (2 * RING)
    first = y + core * (z - y)
    second = z + core * (y - z)

    def device(index):
        index = lax.rem(index + devices, devices)
        return (index // 4, lax.rem(index, 4))

    def chip(a, b):
        a = lax.rem(a + RING, RING)
        b = lax.rem(b + RING, RING)
        row = a + core * (b - a)
        layer = b + core * (a - b)
        return ((layer * RING + row) * 2 + core, sub)

    ahead, behind = chip(first + 1, second), chip(first - 1, second)
    right, left = chip(first, second + 1), chip(first, second - 1)
    sibling = (leaf + 1 - 2 * core, sub)

    def load(source, target, index):
        copy = pltpu.make_async_copy(source, target, load_sem.at[index])
        copy.start()
        return copy

    light_loads = [
        load(light_hbm.at[:, pl.ds(t * LEAF, LEAF)], window.at[HALO + t], 4 + t) for t in range(LEAVES)
    ]
    basis_load = load(basis_hbm, basis, 1)
    transfer_load = load(transfer_hbm, transfer, 2)
    coupling_load = load(coupling_hbm, coupling, 3)

    barrier = pltpu.get_barrier_semaphore()
    friends = [device(me + s * k) for k in (1, 2, 4, 8, 16) for s in (1, -1)]
    friends += [ahead, behind, right, left]
    for friend in friends:
        pl.semaphore_signal(barrier, inc=1, device_id=friend, device_id_type=MESH)

    geo[HALO : HALO + LEAVES] = jnp.zeros((LEAVES, 8, LEAF), F32)
    for t in range(LEAVES):
        geo[HALO + t, 0:4, :] = probes_ref[:, t * LEAF : (t + 1) * LEAF].astype(F32)
    lanes = lax.broadcasted_iota(jnp.int32, (LIGHTS, 2 * RANK), 1)
    mask[0] = jnp.where(lanes < RANK, 1.0, 0.0).astype(BF16)
    mask[1] = jnp.where(lanes < RANK, 0.0, 1.0).astype(BF16)

    pl.semaphore_wait(barrier, len(friends))

    def send(source, target, send_sem, recv_sem, to):
        return pltpu.make_async_remote_copy(
            src_ref=source,
            dst_ref=target,
            send_sem=send_sem,
            recv_sem=recv_sem,
            device_id=to,
            device_id_type=MESH,
        )

    pending = []

    def halo(ref, index):
        down = send(
            ref.at[pl.ds(HALO, HALO)],
            ref.at[pl.ds(HALO + LEAVES, HALO)],
            halo_send.at[index],
            halo_recv.at[index],
            device(me - 1),
        )
        up = send(
            ref.at[pl.ds(LEAVES, HALO)],
            ref.at[pl.ds(0, HALO)],
            halo_send.at[index + 1],
            halo_recv.at[index + 1],
            device(me + 1),
        )
        down.start()
        up.start()
        return [down, up]

    halos = halo(geo, 0)
    for light_load in light_loads:
        light_load.wait()
    basis_load.wait()

    chip_place = z * RING + y
    my_block = (core * LINE + chip_place) * PER_CHIP
    pairs = []
    for q in range(LEAVES // 2):
        parts = []
        for t in (2 * q, 2 * q + 1):
            parts.append(lax.dot_general(window[HALO + t], basis[t], NT, preferred_element_type=F32))
        pairs.append(jnp.concatenate(parts, axis=1).astype(BF16))
    for i in range(2):
        lower, higher = pairs[i], pairs[2 + i]
        pool[my_block + core * 2 + i] = jnp.where(core == 0, lower.astype(F32), higher.astype(F32)).astype(BF16)
        traded[i] = jnp.where(core == 0, higher.astype(F32), lower.astype(F32)).astype(BF16)
    other_block = ((1 - core) * LINE + chip_place) * PER_CHIP
    trade = send(
        traded,
        pool.at[pl.ds(other_block + core * 2, 2)],
        trade_send,
        trade_recv,
        sibling,
    )
    trade.start()
    pending.append(trade)
    halos += halo(window, 2)

    transfer_load.wait()
    stacked = jnp.concatenate(pairs, axis=1)
    level0 = jnp.dot(stacked, transfer[...], preferred_element_type=F32)

    def twice(value):
        return jnp.concatenate([value, value], axis=1)

    def matrix(value):
        return value.astype(F32)

    def climb(height, value):
        upward[height] = twice(value)
        stride = 2 ** (height + 1)
        moves = [
            send(
                upward.at[height],
                below.at[height],
                tree_send.at[3 * height],
                tree_recv.at[3 * height],
                device(me + stride),
            ),
            send(
                upward.at[height],
                above.at[height],
                tree_send.at[3 * height + 1],
                tree_recv.at[3 * height + 1],
                device(me - stride),
            ),
        ]
        if height < UPLV:
            parity = (me // 2**height) % 2
            mine[height] = twice(
                jnp.dot(value, matrix(up_ref[height, parity]), precision=HIGH, preferred_element_type=F32)
            )
            swap = send(
                mine.at[height],
                partner.at[height],
                tree_send.at[3 * height + 2],
                tree_recv.at[3 * height + 2],
                device(me + (1 - 2 * parity) * 2**height),
            )
            swap.start()
            moves.append(swap)
        moves[0].start()
        moves[1].start()
        return moves

    tree = [climb(0, level0)]

    half_base = core * LINE

    def block(a, b, count=PER_CHIP, skip=0):
        a = lax.rem(a + 2 * RING, RING)
        b = lax.rem(b + 2 * RING, RING)
        row, layer = a + core * (b - a), b + core * (a - b)
        return pool.at[pl.ds((half_base + layer * RING + row) * PER_CHIP + skip, count)]

    def line_copy(j, to):
        ref = block(first + offset_of(j), second)
        return send(ref, ref, line_send.at[j - 1], line_recv.at[j - 1], to)

    def ring_block(n, sign):
        return block(first + offset_of(n % RING), second - sign * (n // RING))

    def to_second(j):
        ref = block(first + offset_of(j), second)
        for sems, to in (
            ((right_send, right_recv), right),
            ((left_send, left_recv), left),
        ):
            send(ref, ref, sems[0].at[j], sems[1].at[j], to).start()
        send(ref, ref, sib_send.at[j], sib_recv.at[j], sibling).start()

    def line_send_of(j, hop, to):
        ref = block(first + offset_of(j), second)
        copy = send(ref, ref, line_send.at[hop - 1], line_recv.at[hop - 1], to)
        copy.start()
        pending_line.append(copy)

    pending_line = []
    trade.wait_recv()
    line_send_of(0, 1, ahead)
    line_send_of(0, 2, behind)
    to_second(0)

    def spread_columns(t):
        turned = jnp.transpose(geo[HALO + t])
        for k in range(4):
            value = turned[:, k : k + 1]
            if k == 3:
                value = value * soften
            columns[t, k] = jnp.broadcast_to(value, (LEAF, 128))

    for t in range(LEAVES):
        near_terms[t] = jnp.zeros((LIGHTS, LEAF), F32)

    def rejoin(height):
        tree[height][2].wait_recv()
        total = mine[height] + partner[height]
        tree.append(climb(height + 1, total[:, :RANK]))

    for j in range(1, RING):
        spread_columns(j - 1)
        if j == RING - 1:
            spread_columns(j)
        if j in (2, 4, 6):
            rejoin(j // 2 - 1)
        arrived = line_copy(j, ahead)
        arrived.wait_recv()
        hop = (j + 1) // 2
        if j % 2 == 1 and hop < RING // 2:
            line_send_of(j, j + 2, ahead)
        if j % 2 == 0 and hop < RING // 2 - 1:
            line_send_of(j, j + 2, behind)
        to_second(j)

    for move in halos:
        move.wait_recv()

    def near_pair(p):
        t, k = p // (NNEAR + 1), p % (NNEAR + 1)
        named = (near_list_ref[jnp.maximum(k - 1, 0), t] - LEAVES * me + HALO) & (LEAVES + 2 * HALO - 1)
        w = jnp.where(k == 0, t + HALO, named)
        shift = (t + HALO - w).astype(F32) * spacing
        rows = geo[w]
        row_x, row_y, row_z, row_a = (rows[0:1] - shift, rows[1:2], rows[2:3], rows[3:4])
        for i in range(0, LEAF, 32):
            sides = []
            for lane in (0, 128):
                cut = slice(lane, lane + 128)
                dx = columns[t, 0, i : i + 32] - row_x[:, cut]
                dy = columns[t, 1, i : i + 32] - row_y[:, cut]
                dz = columns[t, 2, i : i + 32] - row_z[:, cut]
                total = dx * dx + soften + dy * dy + dz * dz
                guess = pl.reciprocal(total, approx=True)
                guess = guess * (2.0 - total * guess)
                sides.append((columns[t, 3, i : i + 32] * row_a[:, cut] * guess).astype(BF16))
            tile[i : i + 32, :] = jnp.concatenate(sides, axis=1)
        near_terms[t] += lax.dot_general(window[w], tile[...], NT, preferred_element_type=F32)

    sides = (
        (1, right, right_send, right_recv, 0),
        (-1, left, left_send, left_recv, 2),
    )

    def half_block(n, sign, skip):
        return block(first + offset_of(n % RING), second - sign * (n // RING), 2, skip)

    def whole_step(n, carry):
        for side, (sign, to, send_sem, recv_sem, skip) in enumerate(sides):
            ref = block(first + offset_of(n % RING), second - sign * (n // RING + 1))
            send(ref, ref, send_sem.at[n], recv_sem.at[n], to).wait_recv()
            send(ref, ref, send_sem.at[n + RING], recv_sem.at[n + RING], to).start()
            index = RING + side * STEPS + n
            send(ref, ref, sib_send.at[index], sib_recv.at[index], sibling).start()
        near_pair(2 * n)
        near_pair(2 * n + 1)
        return carry

    def half_step(n, carry):
        for side, (sign, to, send_sem, recv_sem, skip) in enumerate(sides):
            a, b = first + offset_of(n % RING), second - sign * (n // RING + 1)
            ref, part = block(a, b), block(a, b, 2, skip)
            send(ref, ref, send_sem.at[n], recv_sem.at[n], to).wait_recv()
            send(part, part, send_sem.at[n + RING], recv_sem.at[n + RING], to).start()
            index = RING + side * STEPS + n
            send(ref, ref, sib_send.at[index], sib_recv.at[index], sibling).start()
        near_pair(WHOLE + n)
        return carry

    def last_step(n, carry):
        for side, (sign, to, send_sem, recv_sem, skip) in enumerate(sides):
            a, b = first + offset_of(n % RING), second - sign * (n // RING + 1)
            part = block(a, b, 2, skip)
            send(part, part, send_sem.at[n], recv_sem.at[n], to).wait_recv()
            index = RING + side * STEPS + n
            send(part, part, sib_send.at[index], sib_recv.at[index], sibling).start()
        return carry

    lax.fori_loop(0, WHOLE, whole_step, 0)
    lax.fori_loop(WHOLE, HALVES, half_step, 0)

    downward = None
    for height in range(UPLV, -1, -1):
        tree[height][0].wait_recv()
        tree[height][1].wait_recv()
        cluster = me // 2**height
        low = jnp.where(cluster >= 2, below[height][:, :RANK], 0.0)
        high = jnp.where(cluster + 2 < devices // 2**height, above[height][:, :RANK], 0.0)
        value = jnp.dot(low, matrix(upper_ref[height, 0]), precision=HIGH, preferred_element_type=F32)
        value += jnp.dot(high, matrix(upper_ref[height, 1]), precision=HIGH, preferred_element_type=F32)
        if downward is not None:
            parity = cluster % 2
            value += lax.dot_general(
                downward, matrix(up_ref[height, parity]), NT, precision=HIGH, preferred_element_type=F32
            )
        downward = value
    pulled[...] = lax.dot_general(
        downward, matrix(transfer[...]), NT, precision=HIGH, preferred_element_type=F32
    )

    lax.fori_loop(HALVES, STEPS, last_step, 0)

    coupling_load.wait()

    other_base = (1 - core) * LINE

    def other(a, b, count=PER_CHIP, skip=0):
        a = lax.rem(a + 2 * RING, RING)
        b = lax.rem(b + 2 * RING, RING)
        row, layer = b + core * (a - b), a + core * (b - a)
        return pool.at[pl.ds((other_base + layer * RING + row) * PER_CHIP + skip, count)]

    def wait_own(j, carry):
        ref = other(second + offset_of(j), first)
        send(ref, ref, sib_send.at[j], sib_recv.at[j], sibling).wait_recv()
        return carry

    def wait_whole(n, carry):
        for side, (sign, to, send_sem, recv_sem, skip) in enumerate(sides):
            ref = other(second + offset_of(n % RING), first - sign * (n // RING + 1))
            index = RING + side * STEPS + n
            send(ref, ref, sib_send.at[index], sib_recv.at[index], sibling).wait_recv()
        return carry

    def wait_part(n, carry):
        for side, (sign, to, send_sem, recv_sem, skip) in enumerate(sides):
            ref = other(second + offset_of(n % RING), first - sign * (n // RING + 1), 2, skip)
            index = RING + side * STEPS + n
            send(ref, ref, sib_send.at[index], sib_recv.at[index], sibling).wait_recv()
        return carry

    lax.fori_loop(0, RING, wait_own, 0)
    lax.fori_loop(0, HALVES, wait_whole, 0)
    lax.fori_loop(HALVES, STEPS, wait_part, 0)

    for t in range(LEAVES):
        picked, weights = [], []
        for c in range(NFAR):
            entry = far_list_ref[t, c]
            group, peer, pair = (entry >> 2) & 1, entry >> 5, (entry >> 1) & 1
            picked.append(pool[group * (LINE * PER_CHIP) + peer * 2 + pair] * mask[entry & 1])
            cut = coupling[t, c * RANK : (c + 1) * RANK, :]
            weights += [cut, cut]
        far = jnp.dot(
            jnp.concatenate(picked, axis=1),
            jnp.concatenate(weights, axis=0),
            preferred_element_type=F32,
        )
        leaf_far = (far + pulled[:, t * RANK : (t + 1) * RANK]).astype(BF16)
        back = jnp.dot(leaf_far, basis[t], preferred_element_type=F32)
        out_ref[:, t * LEAF : (t + 1) * LEAF] = (near_terms[t] + back).astype(BF16)

    trade.wait_send()
    for move in halos + pending_line + [m for moves in tree for m in moves]:
        move.wait_send()

    def sent_first(j, carry):
        ref = block(first + offset_of(j), second)
        for side, (sign, to, send_sem, recv_sem, skip) in enumerate(sides):
            send(ref, ref, send_sem.at[j], recv_sem.at[j], to).wait_send()
        send(ref, ref, sib_send.at[j], sib_recv.at[j], sibling).wait_send()
        return carry

    def sent_whole(n, carry):
        for side, (sign, to, send_sem, recv_sem, skip) in enumerate(sides):
            a, b = first + offset_of(n % RING), second - sign * (n // RING + 1)
            ref = block(a, b)
            send(ref, ref, send_sem.at[n + RING], recv_sem.at[n + RING], to).wait_send()
            index = RING + side * STEPS + n
            send(ref, ref, sib_send.at[index], sib_recv.at[index], sibling).wait_send()
        return carry

    def sent_half(n, carry):
        for side, (sign, to, send_sem, recv_sem, skip) in enumerate(sides):
            a, b = first + offset_of(n % RING), second - sign * (n // RING + 1)
            ref, part = block(a, b), block(a, b, 2, skip)
            send(part, part, send_sem.at[n + RING], recv_sem.at[n + RING], to).wait_send()
            index = RING + side * STEPS + n
            send(ref, ref, sib_send.at[index], sib_recv.at[index], sibling).wait_send()
        return carry

    def sent_part(n, carry):
        for side, (sign, to, send_sem, recv_sem, skip) in enumerate(sides):
            a, b = first + offset_of(n % RING), second - sign * (n // RING + 1)
            part = block(a, b, 2, skip)
            index = RING + side * STEPS + n
            send(part, part, sib_send.at[index], sib_recv.at[index], sibling).wait_send()
        return carry

    lax.fori_loop(0, RING, sent_first, 0)
    lax.fori_loop(0, WHOLE, sent_whole, 0)
    lax.fori_loop(WHOLE, HALVES, sent_half, 0)
    lax.fori_loop(HALVES, STEPS, sent_part, 0)


def solution(mesh):
    devices = mesh.shape["leaf"] * mesh.shape["sub"]

    def per_device(
        light,
        probes,
        near_list,
        far_list,
        leaf_basis,
        leaf_transfer,
        far_coupling,
        up_transfer,
        upper_coupling,
    ):
        any_space = pl.BlockSpec(memory_space=pl.ANY)
        vmem = pl.BlockSpec(memory_space=pltpu.VMEM)
        smem = pl.BlockSpec(memory_space=pltpu.SMEM)
        dma = pltpu.SemaphoreType.DMA
        slots = LEAVES + 2 * HALO
        return pl.pallas_call(
            functools.partial(kernel, devices),
            out_shape=jax.ShapeDtypeStruct((LIGHTS, LEAVES * LEAF), BF16),
            in_specs=[any_space, vmem, smem, smem, any_space, any_space, any_space, vmem, vmem],
            out_specs=vmem,
            scratch_shapes=[
                pltpu.VMEM((slots, LIGHTS, LEAF), BF16),
                pltpu.VMEM((slots, 8, LEAF), F32),
                pltpu.VMEM((LEAVES, 4, LEAF, 128), F32),
                pltpu.VMEM((LEAVES, RANK, LEAF), BF16),
                pltpu.VMEM((LEAVES * RANK, RANK), BF16),
                pltpu.VMEM((LEAVES, NFAR * RANK, RANK), BF16),
                pltpu.VMEM((2 * LINE * PER_CHIP, LIGHTS, 2 * RANK), BF16),
                pltpu.VMEM((2, LIGHTS, 2 * RANK), BF16),
                pltpu.VMEM((LEAVES, LIGHTS, LEAF), F32),
                pltpu.VMEM((LIGHTS, LEAVES * RANK), F32),
                pltpu.VMEM((LEAF, LEAF), BF16),
                pltpu.VMEM((UPLV + 1, LIGHTS, 2 * RANK), F32),
                pltpu.VMEM((UPLV, LIGHTS, 2 * RANK), F32),
                pltpu.VMEM((UPLV, LIGHTS, 2 * RANK), F32),
                pltpu.VMEM((UPLV + 1, LIGHTS, 2 * RANK), F32),
                pltpu.VMEM((UPLV + 1, LIGHTS, 2 * RANK), F32),
                pltpu.VMEM((2, LIGHTS, 2 * RANK), BF16),
                dma((4 + LEAVES,)),
                dma((4,)),
                dma((4,)),
                dma,
                dma,
                dma((RING - 1,)),
                dma((RING - 1,)),
                dma((STEPS,)),
                dma((STEPS,)),
                dma((STEPS,)),
                dma((STEPS,)),
                dma((RING + 2 * STEPS,)),
                dma((RING + 2 * STEPS,)),
                dma((3 * (UPLV + 1),)),
                dma((3 * (UPLV + 1),)),
            ],
            compiler_params=pltpu.CompilerParams(
                collective_id=0, has_side_effects=True, vmem_limit_bytes=56 * 2**20
            ),
        )(
            light,
            probes,
            near_list.T,
            far_list,
            jnp.swapaxes(leaf_basis, 1, 2),
            leaf_transfer.reshape(LEAVES * RANK, RANK),
            far_coupling.reshape(LEAVES, NFAR * RANK, RANK),
            up_transfer,
            upper_coupling,
        )

    return jax.shard_map(
        per_device,
        mesh=mesh,
        in_specs=(
            P(None, ("leaf", "sub")),
            P(None, ("leaf", "sub")),
            P(("leaf", "sub"), None),
            P(("leaf", "sub"), None),
            P(("leaf", "sub"), None, None),
            P(("leaf", "sub"), None, None),
            P(("leaf", "sub"), None, None, None),
            P(),
            P(),
        ),
        out_specs=P(None, ("leaf", "sub")),
        check_vma=False,
    )
```

time: 132 us -> 53.3 us (0.40)
  Pallas kernels: 0 us -> 51.6 us
  starting transfers between devices: 45.1 us -> 0 us
  matrix products: 31.5 us -> 0 us
  waiting for transfers between devices: 25.8 us -> 0 us
  between operations: 14.2 us -> 0.01 us
  local copies, waits for them, and re-layouts: 13.1 us -> 1.57 us
  other arithmetic: 1.75 us -> 0 us
    pallas_call x0 -> x1, Pallas kernels: none -> 51.6 us  [per_device(): pl.pallas_call(functools.partial(kernel, devices), out_shape=jax.ShapeDty...]
    ppermute x13 -> x0, starting transfers between devices: 45.1 us -> none  [the longest x8 26.6 us: passed_along(): lax.ppermute(value, axis, [(source, source + steps) for source in range(l...]
    dot_general x28 -> x0, matrix products: 31.5 us -> none  [the longest x9 23.8 us: per_device(): jnp.einsum('rjl,jil->rji', source_values, kernel_tiles, preferred_element...]
    ppermute x13 -> x0, waiting for transfers between devices: 13.5 us -> none  [the longest x8 10.8 us: passed_along(): lax.ppermute(value, axis, [(source, source + steps) for source in range(l...]
    all_gather x1 -> x0, waiting for transfers between devices: 12.3 us -> none  [per_device(): pooled = lax.all_gather(coeff_flat, 'leaf', axis=0, tiled=True)]
    gather x1 -> x0, local copies, waits for them, and re-layouts: 5.09 us -> none  [per_device(): picked = pooled[peer_row * leaf_count + which_leaf]]
    reshape x3 -> x0, local copies, waits for them, and re-layouts: 3.69 us -> none  [the longest x1 2.19 us: per_device(): picked = picked.reshape(leaf_count, -1, light_rows, rank_size)]
    slice x7 -> x0, local copies, waits for them, and re-layouts: 1.58 us -> none  [the longest x1 0.8 us: per_device(): mine_term = high_product(upward[-1], up_transfer[height][parity])]
  transfers between devices with their start and end apart: 14 -> 0, of which waited for: 7 -> 0; matrix products, arithmetic and copies ran while one was open for 24% -> 0% of each run, Pallas kernels for 0% -> 0%
where the time goes in v1:
time: 53.3 us; the launch traced here: 53.2 us
  Pallas kernels  51.6 us (97%)
  local copies, waits for them, and re-layouts  1.57 us (3%)
    pallas_call x1, Pallas kernels, per_device(): pl.pallas_call(functools.partial(kernel, devices), out_shape=jax.ShapeDty...  51.6 us
    unnamed x1, local copies, waits for them, and re-layouts  1.57 us

profile of v1, /device:TPU:1, one launch (start us, length us, event | category | flops | bytes accessed | tf_op | source)
XLA Modules:
  0.0 53.2 jit_solution(7997107542684558157)
XLA Ops:
  0.0 51.6 %shard_map.91 = bf16[32,2048]{1,0:T(8,128)(2,1)} custom-call(bf16[32,2048]{1,0:T(8,128)(2,1)} %light_hbm.1, bf16[4,2048]{1,0:T(4,128)(2,1)} %probes_ref.1, s32[4,8]{1,0:T(4,128)} %bitcast.7, s32[8,32]{1,0:T(8,128)} %far_list_ref.1, bf16[8,64,256]{2,1,0:T(8,128)(2,1)} %bitcast.5, bf16[512,64]{1,0:T(8,128)(2,1)} %bitcast.6, bf16[8,2048,64]{2,1,0:T(8,128)(2,1)} %bitcast.4, ...), custom_call_target="tpu_custom_call" | custom-call | tf_op jit(solution)/shard_map/pallas_call | solution.py:510
  51.6 1.6 %copy.11 = bf16[32,2048]{1,0:T(8,128)(2,1)} copy(bf16[32,2048]{1,0:T(8,128)(2,1)} %shard_map.91) | data formatting | bytes 262144

commit v2 on v1

v2 whole, which is shorter than its diff:
```python
import functools

import jax
import jax.numpy as jnp
from jax import lax
from jax.experimental import pallas as pl
from jax.experimental.pallas import tpu as pltpu
from jax.sharding import PartitionSpec as P

MESH = pl.DeviceIdType.MESH
F32, BF16 = jnp.float32, jnp.bfloat16

HALO = 4
UPLV = 3
LEAF = 256
RANK = 64
LIGHTS = 32
LEAVES = 8
NNEAR = 4
NFAR = 32
soften = 0.0025
spacing = 0.25

RING = 8
LINE = RING * RING
PER_CHIP = 4
STEPS = RING * RING // 2
WHOLE = 16
HALVES = 24

NEAREST = (0, -1, 1, -2, 2)

NT = (((1,), (1,)), ((), ()))


def offset_of(j):
    return ((j + 1) // 2) * (1 - 2 * (j % 2))


def kernel(
    devices,
    light_hbm,
    probes_ref,
    near_list_ref,
    far_list_ref,
    basis_hbm,
    transfer_hbm,
    coupling_hbm,
    up_ref,
    upper_ref,
    out_ref,
    window,
    geo,
    columns,
    basis,
    transfer,
    coupling,
    pool,
    traded,
    near_terms,
    pulled,
    tile,
    upward,
    mine,
    partner,
    below,
    above,
    mask,
    load_sem,
    halo_send,
    halo_recv,
    first_send,
    first_recv,
    right_send,
    right_recv,
    left_send,
    left_recv,
    sib_send,
    sib_recv,
    tree_send,
    tree_recv,
):
    leaf = lax.axis_index("leaf")
    sub = lax.axis_index("sub")
    me = leaf * 4 + sub
    core = leaf % 2
    y = (leaf // 2) % RING
    z = leaf // (2 * RING)
    first = y + core * (z - y)
    second = z + core * (y - z)

    def device(index):
        index = lax.rem(index + devices, devices)
        return (index // 4, lax.rem(index, 4))

    def chip(a, b):
        a = lax.rem(a + RING, RING)
        b = lax.rem(b + RING, RING)
        row = a + core * (b - a)
        layer = b + core * (a - b)
        return ((layer * RING + row) * 2 + core, sub)

    def across(a, b):
        to_leaf, to_sub = chip(a, b)
        return (to_leaf + 1 - 2 * core, to_sub)

    right, left = chip(first, second + 1), chip(first, second - 1)
    sibling = (leaf + 1 - 2 * core, sub)

    def load(source, target, index):
        copy = pltpu.make_async_copy(source, target, load_sem.at[index])
        copy.start()
        return copy

    light_loads = [
        load(light_hbm.at[:, pl.ds(t * LEAF, LEAF)], window.at[HALO + t], 4 + t) for t in range(LEAVES)
    ]
    basis_load = load(basis_hbm, basis, 1)
    transfer_load = load(transfer_hbm, transfer, 2)
    coupling_load = load(coupling_hbm, coupling, 3)

    barrier = pltpu.get_barrier_semaphore()
    friends = [device(me + s * k) for k in (1, 2, 4, 8, 16) for s in (1, -1)]
    friends += [right, left]
    friends += [chip(first + k, second) for k in NEAREST if k]
    friends += [across(first + k, second) for k in NEAREST]
    for friend in friends:
        pl.semaphore_signal(barrier, inc=1, device_id=friend, device_id_type=MESH)

    geo[HALO : HALO + LEAVES] = jnp.zeros((LEAVES, 8, LEAF), F32)
    for t in range(LEAVES):
        geo[HALO + t, 0:4, :] = probes_ref[:, t * LEAF : (t + 1) * LEAF].astype(F32)
    lanes = lax.broadcasted_iota(jnp.int32, (LIGHTS, 2 * RANK), 1)
    mask[0] = jnp.where(lanes < RANK, 1.0, 0.0).astype(BF16)
    mask[1] = jnp.where(lanes < RANK, 0.0, 1.0).astype(BF16)

    def send(source, target, send_sem, recv_sem, to):
        return pltpu.make_async_remote_copy(
            src_ref=source,
            dst_ref=target,
            send_sem=send_sem,
            recv_sem=recv_sem,
            device_id=to,
            device_id_type=MESH,
        )

    def halo(ref, index):
        down = send(
            ref.at[pl.ds(HALO, HALO)],
            ref.at[pl.ds(HALO + LEAVES, HALO)],
            halo_send.at[index],
            halo_recv.at[index],
            device(me - 1),
        )
        up = send(
            ref.at[pl.ds(LEAVES, HALO)],
            ref.at[pl.ds(0, HALO)],
            halo_send.at[index + 1],
            halo_recv.at[index + 1],
            device(me + 1),
        )
        down.start()
        up.start()
        return [down, up]

    for light_load in light_loads:
        light_load.wait()
    basis_load.wait()

    chip_place = z * RING + y
    my_block = (core * LINE + chip_place) * PER_CHIP
    pairs = []
    for q in range(LEAVES // 2):
        parts = []
        for t in (2 * q, 2 * q + 1):
            parts.append(lax.dot_general(window[HALO + t], basis[t], NT, preferred_element_type=F32))
        pairs.append(jnp.concatenate(parts, axis=1).astype(BF16))
    for i in range(2):
        lower, higher = pairs[i], pairs[2 + i]
        pool[my_block + core * 2 + i] = jnp.where(core == 0, lower.astype(F32), higher.astype(F32)).astype(BF16)
        traded[i] = jnp.where(core == 0, higher.astype(F32), lower.astype(F32)).astype(BF16)
    other_block = ((1 - core) * LINE + chip_place) * PER_CHIP

    pl.semaphore_wait(barrier, len(friends))

    for j, k in enumerate(NEAREST):
        theirs = pool.at[pl.ds(other_block + core * 2, 2)]
        send(traded, theirs, first_send, first_recv.at[j], across(first, second - k)).start()
        if k:
            ours = pool.at[pl.ds(my_block + core * 2, 2)]
            send(ours, ours, first_send, first_recv.at[j], chip(first - k, second)).start()
    halos = halo(geo, 0) + halo(window, 2)

    transfer_load.wait()
    stacked = jnp.concatenate(pairs, axis=1)
    level0 = jnp.dot(stacked, transfer[...], preferred_element_type=F32)

    def twice(value):
        return jnp.concatenate([value, value], axis=1)

    def exact(value, matrix, dims=(((1,), (0,)), ((), ()))):
        high = value.astype(BF16)
        rest = value - high.astype(F32)
        middle = rest.astype(BF16)
        low = (rest - middle.astype(F32)).astype(BF16)
        parts = jnp.concatenate([high, middle, low], axis=0)
        product = lax.dot_general(parts, matrix, dims, preferred_element_type=F32)
        return product[:LIGHTS] + (product[LIGHTS : 2 * LIGHTS] + product[2 * LIGHTS :])

    def climb(height, value):
        upward[height] = twice(value)
        stride = 2 ** (height + 1)
        moves = [
            send(
                upward.at[height],
                below.at[height],
                tree_send.at[3 * height],
                tree_recv.at[3 * height],
                device(me + stride),
            ),
            send(
                upward.at[height],
                above.at[height],
                tree_send.at[3 * height + 1],
                tree_recv.at[3 * height + 1],
                device(me - stride),
            ),
        ]
        if height < UPLV:
            parity = (me // 2**height) % 2
            mine[height] = twice(exact(value, up_ref[height, parity]))
            swap = send(
                mine.at[height],
                partner.at[height],
                tree_send.at[3 * height + 2],
                tree_recv.at[3 * height + 2],
                device(me + (1 - 2 * parity) * 2**height),
            )
            swap.start()
            moves.append(swap)
        moves[0].start()
        moves[1].start()
        return moves

    tree = [climb(0, level0)]

    half_base = core * LINE

    def block(a, b, count=PER_CHIP, skip=0):
        a = lax.rem(a + 2 * RING, RING)
        b = lax.rem(b + 2 * RING, RING)
        row, layer = a + core * (b - a), b + core * (a - b)
        return pool.at[pl.ds((half_base + layer * RING + row) * PER_CHIP + skip, count)]

    def to_second(j):
        ref = block(first + offset_of(j), second)
        for send_sem, recv_sem, to in (
            (right_send, right_recv, right),
            (left_send, left_recv, left),
        ):
            send(ref, ref, send_sem, recv_sem.at[j], to).start()
        send(ref, ref, sib_send, sib_recv, sibling).start()

    def arrive(j):
        ref = block(first + offset_of(j), second)
        if j == 0:
            ref = block(first, second, 2)
        send(ref, ref, first_send, first_recv.at[j], sibling).wait_recv()

    def pass_on(j, later, to):
        ref = block(first + offset_of(j), second)
        send(ref, ref, first_send, first_recv.at[later], to).start()

    def spread_columns(t):
        turned = jnp.transpose(geo[HALO + t])
        for k in range(4):
            value = turned[:, k : k + 1]
            if k == 3:
                value = value * soften
            columns[t, k] = jnp.broadcast_to(value, (LEAF, 128))

    def add_tile(t, w, shift, before):
        rows = geo[w]
        row_x, row_y, row_z, row_a = (rows[0:1] - shift, rows[1:2], rows[2:3], rows[3:4])
        for i in range(0, LEAF, 32):
            sides = []
            for lane in (0, 128):
                cut = slice(lane, lane + 128)
                dx = columns[t, 0, i : i + 32] - row_x[:, cut]
                dy = columns[t, 1, i : i + 32] - row_y[:, cut]
                dz = columns[t, 2, i : i + 32] - row_z[:, cut]
                total = dx * dx + soften + dy * dy + dz * dz
                guess = pl.reciprocal(total, approx=True)
                guess = guess * (2.0 - total * guess)
                sides.append((columns[t, 3, i : i + 32] * row_a[:, cut] * guess).astype(BF16))
            tile[i : i + 32, :] = jnp.concatenate(sides, axis=1)
        near_terms[t] = before + lax.dot_general(window[w], tile[...], NT, preferred_element_type=F32)

    def near_self(t, carry):
        add_tile(t, HALO + t, 0.0, 0.0)
        return carry

    def near_pair(p):
        t, k = p // NNEAR, p % NNEAR
        w = (near_list_ref[k, t] - LEAVES * me + HALO) & (LEAVES + 2 * HALO - 1)
        add_tile(t, w, (t + HALO - w).astype(F32) * spacing, near_terms[t])

    for t in range(LEAVES):
        spread_columns(t)

    for j in range(5):
        arrive(j)
        if j == 3:
            pass_on(3, 5, chip(first + 1, second))
            pass_on(3, 7, chip(first + 2, second))
        if j == 4:
            pass_on(4, 6, chip(first - 1, second))
        to_second(j)
    lax.fori_loop(0, LEAVES // 2, near_self, 0)
    for j in range(5, RING):
        arrive(j)
        to_second(j)
    lax.fori_loop(LEAVES // 2, LEAVES, near_self, 0)

    def rejoin(height):
        tree[height][2].wait_recv()
        total = mine[height] + partner[height]
        tree.append(climb(height + 1, total[:, :RANK]))

    for move in halos:
        move.wait_recv()

    sides = (
        (1, right, right_send, right_recv, 0),
        (-1, left, left_send, left_recv, 2),
    )

    def whole_step(n, carry):
        for sign, to, send_sem, recv_sem, skip in sides:
            ref = block(first + offset_of(n % RING), second - sign * (n // RING + 1))
            send(ref, ref, send_sem, recv_sem.at[n], to).wait_recv()
            send(ref, ref, send_sem, recv_sem.at[n + RING], to).start()
            send(ref, ref, sib_send, sib_recv, sibling).start()
        near_pair(n)
        return carry

    def half_step(n, carry):
        for sign, to, send_sem, recv_sem, skip in sides:
            a, b = first + offset_of(n % RING), second - sign * (n // RING + 1)
            ref, part = block(a, b), block(a, b, 2, skip)
            send(ref, ref, send_sem, recv_sem.at[n], to).wait_recv()
            send(part, part, send_sem, recv_sem.at[n + RING], to).start()
            send(ref, ref, sib_send, sib_recv, sibling).start()
        near_pair(n)
        return carry

    def last_step(n, carry):
        for sign, to, send_sem, recv_sem, skip in sides:
            a, b = first + offset_of(n % RING), second - sign * (n // RING + 1)
            part = block(a, b, 2, skip)
            send(part, part, send_sem, recv_sem.at[n], to).wait_recv()
            send(part, part, sib_send, sib_recv, sibling).start()
        near_pair(n)
        return carry

    done = 0
    for height in range(UPLV):
        lax.fori_loop(done, 4 * height + 2, whole_step, 0)
        done = 4 * height + 2
        rejoin(height)
    lax.fori_loop(done, WHOLE, whole_step, 0)
    lax.fori_loop(WHOLE, HALVES, half_step, 0)

    downward = None
    for height in range(UPLV, -1, -1):
        tree[height][0].wait_recv()
        tree[height][1].wait_recv()
        cluster = me // 2**height
        low = jnp.where(cluster >= 2, below[height][:, :RANK], 0.0)
        high = jnp.where(cluster + 2 < devices // 2**height, above[height][:, :RANK], 0.0)
        value = exact(low, upper_ref[height, 0]) + exact(high, upper_ref[height, 1])
        if downward is not None:
            value += exact(downward, up_ref[height, cluster % 2], NT)
        downward = value
    pulled[...] = exact(downward, transfer[...], NT)

    lax.fori_loop(HALVES, STEPS, last_step, 0)

    coupling_load.wait()

    others = pool.at[pl.ds((1 - core) * LINE * PER_CHIP, LINE * PER_CHIP)]
    send(others, others, sib_send, sib_recv, sibling).wait_recv()

    for t in range(LEAVES):
        picked, weights = [], []
        for c in range(NFAR):
            entry = far_list_ref[t, c]
            group, peer, pair = (entry >> 2) & 1, entry >> 5, (entry >> 1) & 1
            picked.append(pool[group * (LINE * PER_CHIP) + peer * 2 + pair] * mask[entry & 1])
            cut = coupling[t, c * RANK : (c + 1) * RANK, :]
            weights += [cut, cut]
        far = jnp.dot(
            jnp.concatenate(picked, axis=1),
            jnp.concatenate(weights, axis=0),
            preferred_element_type=F32,
        )
        leaf_far = (far + pulled[:, t * RANK : (t + 1) * RANK]).astype(BF16)
        back = jnp.dot(leaf_far, basis[t], preferred_element_type=F32)
        out_ref[:, t * LEAF : (t + 1) * LEAF] = (near_terms[t] + back).astype(BF16)

    for move in halos + [m for moves in tree for m in moves]:
        move.wait_send()

    def sent(count, send_sem):
        ref = pool.at[pl.ds(0, count)]
        send(ref, ref, send_sem, sib_recv, sibling).wait_send()

    sent(2 * (2 * len(NEAREST) - 1) + 3 * PER_CHIP, first_send)
    sent(HALVES * PER_CHIP + (STEPS - HALVES) * 2, right_send)
    sent(HALVES * PER_CHIP + (STEPS - HALVES) * 2, left_send)
    sent(LINE * PER_CHIP, sib_send)


def solution(mesh):
    devices = mesh.shape["leaf"] * mesh.shape["sub"]

    def per_device(
        light,
        probes,
        near_list,
        far_list,
        leaf_basis,
        leaf_transfer,
        far_coupling,
        up_transfer,
        upper_coupling,
    ):
        any_space = pl.BlockSpec(memory_space=pl.ANY)
        vmem = pl.BlockSpec(memory_space=pltpu.VMEM)
        smem = pl.BlockSpec(memory_space=pltpu.SMEM)
        dma = pltpu.SemaphoreType.DMA
        slots = LEAVES + 2 * HALO
        return pl.pallas_call(
            functools.partial(kernel, devices),
            out_shape=jax.ShapeDtypeStruct((LIGHTS, LEAVES * LEAF), BF16),
            in_specs=[any_space, vmem, smem, smem, any_space, any_space, any_space, vmem, vmem],
            out_specs=vmem,
            scratch_shapes=[
                pltpu.VMEM((slots, LIGHTS, LEAF), BF16),
                pltpu.VMEM((slots, 8, LEAF), F32),
                pltpu.VMEM((LEAVES, 4, LEAF, 128), F32),
                pltpu.VMEM((LEAVES, RANK, LEAF), BF16),
                pltpu.VMEM((LEAVES * RANK, RANK), BF16),
                pltpu.VMEM((LEAVES, NFAR * RANK, RANK), BF16),
                pltpu.VMEM((2 * LINE * PER_CHIP, LIGHTS, 2 * RANK), BF16),
                pltpu.VMEM((2, LIGHTS, 2 * RANK), BF16),
                pltpu.VMEM((LEAVES, LIGHTS, LEAF), F32),
                pltpu.VMEM((LIGHTS, LEAVES * RANK), F32),
                pltpu.VMEM((LEAF, LEAF), BF16),
                pltpu.VMEM((UPLV + 1, LIGHTS, 2 * RANK), F32),
                pltpu.VMEM((UPLV, LIGHTS, 2 * RANK), F32),
                pltpu.VMEM((UPLV, LIGHTS, 2 * RANK), F32),
                pltpu.VMEM((UPLV + 1, LIGHTS, 2 * RANK), F32),
                pltpu.VMEM((UPLV + 1, LIGHTS, 2 * RANK), F32),
                pltpu.VMEM((2, LIGHTS, 2 * RANK), BF16),
                dma((4 + LEAVES,)),
                dma((4,)),
                dma((4,)),
                dma,
                dma((RING,)),
                dma,
                dma((STEPS,)),
                dma,
                dma((STEPS,)),
                dma,
                dma,
                dma((3 * (UPLV + 1),)),
                dma((3 * (UPLV + 1),)),
            ],
            compiler_params=pltpu.CompilerParams(
                collective_id=0, has_side_effects=True, vmem_limit_bytes=56 * 2**20
            ),
        )(
            light,
            probes,
            near_list.T,
            far_list,
            jnp.swapaxes(leaf_basis, 1, 2),
            leaf_transfer.reshape(LEAVES * RANK, RANK),
            far_coupling.reshape(LEAVES, NFAR * RANK, RANK),
            up_transfer,
            upper_coupling,
        )

    return jax.shard_map(
        per_device,
        mesh=mesh,
        in_specs=(
            P(None, ("leaf", "sub")),
            P(None, ("leaf", "sub")),
            P(("leaf", "sub"), None),
            P(("leaf", "sub"), None),
            P(("leaf", "sub"), None, None),
            P(("leaf", "sub"), None, None),
            P(("leaf", "sub"), None, None, None),
            P(),
            P(),
        ),
        out_specs=P(None, ("leaf", "sub")),
        check_vma=False,
    )
```

time: 53.3 us -> 47.4 us (0.89)
  Pallas kernels: 51.6 us -> 45.7 us
    pallas_call x1, Pallas kernels: 51.6 us -> 45.7 us  [per_device(): pl.pallas_call(functools.partial(kernel, devices), out_shape=jax.ShapeDty...]
where the time goes in v2:
time: 47.4 us; the launch traced here: 47.3 us
  Pallas kernels  45.7 us (96%)
  local copies, waits for them, and re-layouts  1.57 us (3%)
    pallas_call x1, Pallas kernels, per_device(): pl.pallas_call(functools.partial(kernel, devices), out_shape=jax.ShapeDty...  45.7 us
    unnamed x1, local copies, waits for them, and re-layouts  1.57 us

profile of v2, /device:TPU:1, one launch (start us, length us, event | category | flops | bytes accessed | tf_op | source)
XLA Modules:
  0.0 47.3 jit_solution(11987167595022992747)
XLA Ops:
  0.0 45.7 %shard_map.91 = bf16[32,2048]{1,0:T(8,128)(2,1)} custom-call(bf16[32,2048]{1,0:T(8,128)(2,1)} %light_hbm.1, bf16[4,2048]{1,0:T(4,128)(2,1)} %probes_ref.1, s32[4,8]{1,0:T(4,128)} %bitcast.7, s32[8,32]{1,0:T(8,128)} %far_list_ref.1, bf16[8,64,256]{2,1,0:T(8,128)(2,1)} %bitcast.5, bf16[512,64]{1,0:T(8,128)(2,1)} %bitcast.6, bf16[8,2048,64]{2,1,0:T(8,128)(2,1)} %bitcast.4, ...), custom_call_target="tpu_custom_call" | custom-call | tf_op jit(solution)/shard_map/pallas_call | solution.py:443
  45.7 1.6 %copy.11 = bf16[32,2048]{1,0:T(8,128)(2,1)} copy(bf16[32,2048]{1,0:T(8,128)(2,1)} %shard_map.91) | data formatting | bytes 262144

commit v3 on v2

--- a/solution.py
+++ b/solution.py
@@ -24,17 +24,13 @@
 RING = 8
 LINE = RING * RING
 PER_CHIP = 4
-STEPS = RING * RING // 2
-WHOLE = 16
-HALVES = 24
-
-NEAREST = (0, -1, 1, -2, 2)
+CHUNKS = 4
+CHUNK = RING // CHUNKS * PER_CHIP
+STEPS = RING // 2 * CHUNKS - CHUNKS // 2
+PASSED = STEPS - CHUNKS
+TILES = 3
 
 NT = (((1,), (1,)), ((), ()))
-
-
-def offset_of(j):
-    return ((j + 1) // 2) * (1 - 2 * (j % 2))
 
 
 def kernel(
@@ -66,6 +62,7 @@
     below,
     above,
     mask,
+    codes,
     load_sem,
     halo_send,
     halo_recv,
@@ -122,8 +119,8 @@
     barrier = pltpu.get_barrier_semaphore()
     friends = [device(me + s * k) for k in (1, 2, 4, 8, 16) for s in (1, -1)]
     friends += [right, left]
-    friends += [chip(first + k, second) for k in NEAREST if k]
-    friends += [across(first + k, second) for k in NEAREST]
+    friends += [chip(first + k, second) for k in range(1, RING)]
+    friends += [across(first + k, second) for k in range(RING)]
     for friend in friends:
         pl.semaphore_signal(barrier, inc=1, device_id=friend, device_id_type=MESH)
 
@@ -167,8 +164,7 @@
         light_load.wait()
     basis_load.wait()
 
-    chip_place = z * RING + y
-    my_block = (core * LINE + chip_place) * PER_CHIP
+    my_block = (core * LINE + second * RING + first) * PER_CHIP + core * 2
     pairs = []
     for q in range(LEAVES // 2):
         parts = []
@@ -177,18 +173,17 @@
         pairs.append(jnp.concatenate(parts, axis=1).astype(BF16))
     for i in range(2):
         lower, higher = pairs[i], pairs[2 + i]
-        pool[my_block + core * 2 + i] = jnp.where(core == 0, lower.astype(F32), higher.astype(F32)).astype(BF16)
+        pool[my_block + i] = jnp.where(core == 0, lower.astype(F32), higher.astype(F32)).astype(BF16)
         traded[i] = jnp.where(core == 0, higher.astype(F32), lower.astype(F32)).astype(BF16)
-    other_block = ((1 - core) * LINE + chip_place) * PER_CHIP
+    other_block = ((1 - core) * LINE + first * RING + second) * PER_CHIP + core * 2
 
     pl.semaphore_wait(barrier, len(friends))
 
-    for j, k in enumerate(NEAREST):
-        theirs = pool.at[pl.ds(other_block + core * 2, 2)]
-        send(traded, theirs, first_send, first_recv.at[j], across(first, second - k)).start()
+    ours, theirs = pool.at[pl.ds(my_block, 2)], pool.at[pl.ds(other_block, 2)]
+    for k in range(RING):
+        send(traded, theirs, first_send, first_recv.at[second // 2], across(first, second + k)).start()
         if k:
-            ours = pool.at[pl.ds(my_block + core * 2, 2)]
-            send(ours, ours, first_send, first_recv.at[j], chip(first - k, second)).start()
+            send(ours, ours, first_send, first_recv.at[first // 2], chip(first + k, second)).start()
     halos = halo(geo, 0) + halo(window, 2)
 
     transfer_load.wait()
@@ -244,32 +239,26 @@
 
     tree = [climb(0, level0)]
 
-    half_base = core * LINE
-
-    def block(a, b, count=PER_CHIP, skip=0):
-        a = lax.rem(a + 2 * RING, RING)
-        b = lax.rem(b + 2 * RING, RING)
-        row, layer = a + core * (b - a), b + core * (a - b)
-        return pool.at[pl.ds((half_base + layer * RING + row) * PER_CHIP + skip, count)]
-
-    def to_second(j):
-        ref = block(first + offset_of(j), second)
-        for send_sem, recv_sem, to in (
-            (right_send, right_recv, right),
-            (left_send, left_recv, left),
-        ):
-            send(ref, ref, send_sem, recv_sem.at[j], to).start()
+    def chunk(n, sign):
+        b = lax.rem(second - sign * (n // CHUNKS) + RING, RING)
+        q = lax.rem(first // 2 + n + (CHUNKS // 2) * (sign < 0) + 2 * RING, CHUNKS)
+        return pool.at[pl.ds((core * LINE + b * RING) * PER_CHIP + q * CHUNK, CHUNK)]
+
+    def arrive(q):
+        at = lax.rem(first // 2 + q, CHUNKS)
+        ref = pool.at[pl.ds(0, CHUNK if q else CHUNK - 2)]
+        send(ref, ref, first_send, first_recv.at[at], sibling).wait_recv()
+
+    def to_right(n):
+        ref = chunk(n, 1)
+        send(ref, ref, right_send, right_recv.at[n], right).start()
+
+    def to_left(n):
+        ref = chunk(n, -1)
+        send(ref, ref, left_send, left_recv.at[n], left).start()
+
+    def to_sibling(ref):
         send(ref, ref, sib_send, sib_recv, sibling).start()
-
-    def arrive(j):
-        ref = block(first + offset_of(j), second)
-        if j == 0:
-            ref = block(first, second, 2)
-        send(ref, ref, first_send, first_recv.at[j], sibling).wait_recv()
-
-    def pass_on(j, later, to):
-        ref = block(first + offset_of(j), second)
-        send(ref, ref, first_send, first_recv.at[later], to).start()
 
     def spread_columns(t):
         turned = jnp.transpose(geo[HALO + t])
@@ -279,7 +268,7 @@
                 value = value * soften
             columns[t, k] = jnp.broadcast_to(value, (LEAF, 128))
 
-    def add_tile(t, w, shift, before):
+    def add_tile(t, w, shift, before, slot):
         rows = geo[w]
         row_x, row_y, row_z, row_a = (rows[0:1] - shift, rows[1:2], rows[2:3], rows[3:4])
         for i in range(0, LEAF, 32):
@@ -293,34 +282,44 @@
                 guess = pl.reciprocal(total, approx=True)
                 guess = guess * (2.0 - total * guess)
                 sides.append((columns[t, 3, i : i + 32] * row_a[:, cut] * guess).astype(BF16))
-            tile[i : i + 32, :] = jnp.concatenate(sides, axis=1)
-        near_terms[t] = before + lax.dot_general(window[w], tile[...], NT, preferred_element_type=F32)
-
-    def near_self(t, carry):
-        add_tile(t, HALO + t, 0.0, 0.0)
-        return carry
-
-    def near_pair(p):
+            tile[slot, i : i + 32, :] = jnp.concatenate(sides, axis=1)
+        near_terms[t] = before + lax.dot_general(window[w], tile[slot], NT, preferred_element_type=F32)
+
+    def near_pair(p, slot):
         t, k = p // NNEAR, p % NNEAR
         w = (near_list_ref[k, t] - LEAVES * me + HALO) & (LEAVES + 2 * HALO - 1)
-        add_tile(t, w, (t + HALO - w).astype(F32) * spacing, near_terms[t])
+        add_tile(t, w, (t + HALO - w).astype(F32) * spacing, near_terms[t], slot)
+
+    def encode(t, carry):
+        for c in range(NFAR):
+            entry = far_list_ref[t, c]
+            layer, row, group = entry >> 9, (entry >> 6) & 7, (entry >> 2) & 1
+            low, high = layer * RING + row, row * RING + layer + LINE
+            place = low + group * (high - low)
+            codes[t, c] = place * 8 + ((entry >> 5) & 1) * 4 + (entry & 3)
+        return carry
 
     for t in range(LEAVES):
         spread_columns(t)
-
-    for j in range(5):
-        arrive(j)
-        if j == 3:
-            pass_on(3, 5, chip(first + 1, second))
-            pass_on(3, 7, chip(first + 2, second))
-        if j == 4:
-            pass_on(4, 6, chip(first - 1, second))
-        to_second(j)
-    lax.fori_loop(0, LEAVES // 2, near_self, 0)
-    for j in range(5, RING):
-        arrive(j)
-        to_second(j)
-    lax.fori_loop(LEAVES // 2, LEAVES, near_self, 0)
+    lax.fori_loop(0, LEAVES, encode, 0)
+    for t in range(LEAVES // 2):
+        add_tile(t, HALO + t, 0.0, 0.0, t % TILES)
+
+    arrive(0)
+    to_right(0)
+    arrive(2)
+    to_left(0)
+    arrive(1)
+    to_right(1)
+    arrive(3)
+    to_left(1)
+    for n in (2, 3):
+        to_right(n)
+        to_left(n)
+    for n in range(CHUNKS):
+        to_sibling(chunk(n, 1))
+    for t in range(LEAVES // 2, LEAVES):
+        add_tile(t, HALO + t, 0.0, 0.0, t % TILES)
 
     def rejoin(height):
         tree[height][2].wait_recv()
@@ -330,46 +329,36 @@
     for move in halos:
         move.wait_recv()
 
-    sides = (
-        (1, right, right_send, right_recv, 0),
-        (-1, left, left_send, left_recv, 2),
-    )
-
-    def whole_step(n, carry):
-        for sign, to, send_sem, recv_sem, skip in sides:
-            ref = block(first + offset_of(n % RING), second - sign * (n // RING + 1))
-            send(ref, ref, send_sem, recv_sem.at[n], to).wait_recv()
-            send(ref, ref, send_sem, recv_sem.at[n + RING], to).start()
-            send(ref, ref, sib_send, sib_recv, sibling).start()
-        near_pair(n)
+    def pass_step(n, carry):
+        ref = chunk(n + CHUNKS, 1)
+        send(ref, ref, right_send, right_recv.at[n], right).wait_recv()
+        send(ref, ref, right_send, right_recv.at[n + CHUNKS], right).start()
+        ref_left = chunk(n + CHUNKS, -1)
+        send(ref_left, ref_left, left_send, left_recv.at[n], left).wait_recv()
+        send(ref_left, ref_left, left_send, left_recv.at[n + CHUNKS], left).start()
+        to_sibling(ref)
+        to_sibling(ref_left)
+        for i in range(TILES):
+            near_pair(TILES * n + i, i)
         return carry
 
-    def half_step(n, carry):
-        for sign, to, send_sem, recv_sem, skip in sides:
-            a, b = first + offset_of(n % RING), second - sign * (n // RING + 1)
-            ref, part = block(a, b), block(a, b, 2, skip)
-            send(ref, ref, send_sem, recv_sem.at[n], to).wait_recv()
-            send(part, part, send_sem, recv_sem.at[n + RING], to).start()
-            send(ref, ref, sib_send, sib_recv, sibling).start()
-        near_pair(n)
-        return carry
-
     def last_step(n, carry):
-        for sign, to, send_sem, recv_sem, skip in sides:
-            a, b = first + offset_of(n % RING), second - sign * (n // RING + 1)
-            part = block(a, b, 2, skip)
-            send(part, part, send_sem, recv_sem.at[n], to).wait_recv()
-            send(part, part, sib_send, sib_recv, sibling).start()
-        near_pair(n)
+        ref = chunk(n + CHUNKS, 1)
+        send(ref, ref, right_send, right_recv.at[n], right).wait_recv()
+        to_sibling(ref)
+        ref_left = chunk(n + CHUNKS, -1)
+        send(ref_left, ref_left, left_send, left_recv.at[n], left).wait_recv()
+        to_sibling(ref_left)
         return carry
 
     done = 0
     for height in range(UPLV):
-        lax.fori_loop(done, 4 * height + 2, whole_step, 0)
-        done = 4 * height + 2
+        lax.fori_loop(done, 3 * height + 2, pass_step, 0)
+        done = 3 * height + 2
         rejoin(height)
-    lax.fori_loop(done, WHOLE, whole_step, 0)
-    lax.fori_loop(WHOLE, HALVES, half_step, 0)
+    lax.fori_loop(done, PASSED, pass_step, 0)
+    for p in range(TILES * PASSED, LEAVES * NNEAR):
+        near_pair(p, p % TILES)
 
     downward = None
     for height in range(UPLV, -1, -1):
@@ -384,7 +373,7 @@
         downward = value
     pulled[...] = exact(downward, transfer[...], NT)
 
-    lax.fori_loop(HALVES, STEPS, last_step, 0)
+    lax.fori_loop(PASSED, STEPS, last_step, 0)
 
     coupling_load.wait()
 
@@ -394,9 +383,8 @@
     for t in range(LEAVES):
         picked, weights = [], []
         for c in range(NFAR):
-            entry = far_list_ref[t, c]
-            group, peer, pair = (entry >> 2) & 1, entry >> 5, (entry >> 1) & 1
-            picked.append(pool[group * (LINE * PER_CHIP) + peer * 2 + pair] * mask[entry & 1])
+            code = codes[t, c]
+            picked.append(pool[code >> 1] * mask[code & 1])
             cut = coupling[t, c * RANK : (c + 1) * RANK, :]
             weights += [cut, cut]
         far = jnp.dot(
@@ -415,9 +403,9 @@
         ref = pool.at[pl.ds(0, count)]
         send(ref, ref, send_sem, sib_recv, sibling).wait_send()
 
-    sent(2 * (2 * len(NEAREST) - 1) + 3 * PER_CHIP, first_send)
-    sent(HALVES * PER_CHIP + (STEPS - HALVES) * 2, right_send)
-    sent(HALVES * PER_CHIP + (STEPS - HALVES) * 2, left_send)
+    sent(2 * (2 * RING - 1), first_send)
+    sent(STEPS * CHUNK, right_send)
+    sent(STEPS * CHUNK, left_send)
     sent(LINE * PER_CHIP, sib_send)
 
 
@@ -456,18 +444,19 @@
                 pltpu.VMEM((2, LIGHTS, 2 * RANK), BF16),
                 pltpu.VMEM((LEAVES, LIGHTS, LEAF), F32),
                 pltpu.VMEM((LIGHTS, LEAVES * RANK), F32),
-                pltpu.VMEM((LEAF, LEAF), BF16),
+                pltpu.VMEM((TILES, LEAF, LEAF), BF16),
                 pltpu.VMEM((UPLV + 1, LIGHTS, 2 * RANK), F32),
                 pltpu.VMEM((UPLV, LIGHTS, 2 * RANK), F32),
                 pltpu.VMEM((UPLV, LIGHTS, 2 * RANK), F32),
                 pltpu.VMEM((UPLV + 1, LIGHTS, 2 * RANK), F32),
                 pltpu.VMEM((UPLV + 1, LIGHTS, 2 * RANK), F32),
                 pltpu.VMEM((2, LIGHTS, 2 * RANK), BF16),
+                pltpu.SMEM((LEAVES, NFAR), jnp.int32),
                 dma((4 + LEAVES,)),
                 dma((4,)),
                 dma((4,)),
                 dma,
-                dma((RING,)),
+                dma((CHUNKS,)),
                 dma,
                 dma((STEPS,)),
                 dma,

time: 47.4 us -> 45.3 us (0.956)
  Pallas kernels: 45.7 us -> 43.6 us
    pallas_call x1, Pallas kernels: 45.7 us -> 43.6 us  [per_device(): pl.pallas_call(functools.partial(kernel, devices), out_shape=jax.ShapeDty...]
where the time goes in v3:
time: 45.3 us; the launch traced here: 45.2 us
  Pallas kernels  43.6 us (96%)
  local copies, waits for them, and re-layouts  1.57 us (3%)
    pallas_call x1, Pallas kernels, per_device(): pl.pallas_call(functools.partial(kernel, devices), out_shape=jax.ShapeDty...  43.6 us
    unnamed x1, local copies, waits for them, and re-layouts  1.57 us

profile of v3, /device:TPU:1, one launch (start us, length us, event | category | flops | bytes accessed | tf_op | source)
XLA Modules:
  0.0 45.2 jit_solution(13951436094546528598)
XLA Ops:
  0.0 43.6 %shard_map.91 = bf16[32,2048]{1,0:T(8,128)(2,1)} custom-call(bf16[32,2048]{1,0:T(8,128)(2,1)} %light_hbm.1, bf16[4,2048]{1,0:T(4,128)(2,1)} %probes_ref.1, s32[4,8]{1,0:T(4,128)} %bitcast.7, s32[8,32]{1,0:T(8,128)} %far_list_ref.1, bf16[8,64,256]{2,1,0:T(8,128)(2,1)} %bitcast.5, bf16[512,64]{1,0:T(8,128)(2,1)} %bitcast.6, bf16[8,2048,64]{2,1,0:T(8,128)(2,1)} %bitcast.4, ...), custom_call_target="tpu_custom_call" | custom-call | tf_op jit(solution)/shard_map/pallas_call | solution.py:431
  43.6 1.6 %copy.11 = bf16[32,2048]{1,0:T(8,128)(2,1)} copy(bf16[32,2048]{1,0:T(8,128)(2,1)} %shard_map.91) | data formatting | bytes 262144

commit v4 on v3

--- a/solution.py
+++ b/solution.py
@@ -27,7 +27,6 @@
 CHUNKS = 4
 CHUNK = RING // CHUNKS * PER_CHIP
 STEPS = RING // 2 * CHUNKS - CHUNKS // 2
-PASSED = STEPS - CHUNKS
 TILES = 3
 
 NT = (((1,), (1,)), ((), ()))
@@ -104,18 +103,6 @@
     right, left = chip(first, second + 1), chip(first, second - 1)
     sibling = (leaf + 1 - 2 * core, sub)
 
-    def load(source, target, index):
-        copy = pltpu.make_async_copy(source, target, load_sem.at[index])
-        copy.start()
-        return copy
-
-    light_loads = [
-        load(light_hbm.at[:, pl.ds(t * LEAF, LEAF)], window.at[HALO + t], 4 + t) for t in range(LEAVES)
-    ]
-    basis_load = load(basis_hbm, basis, 1)
-    transfer_load = load(transfer_hbm, transfer, 2)
-    coupling_load = load(coupling_hbm, coupling, 3)
-
     barrier = pltpu.get_barrier_semaphore()
     friends = [device(me + s * k) for k in (1, 2, 4, 8, 16) for s in (1, -1)]
     friends += [right, left]
@@ -123,6 +110,18 @@
     friends += [across(first + k, second) for k in range(RING)]
     for friend in friends:
         pl.semaphore_signal(barrier, inc=1, device_id=friend, device_id_type=MESH)
+
+    def load(source, target, index):
+        copy = pltpu.make_async_copy(source, target, load_sem.at[index])
+        copy.start()
+        return copy
+
+    light_loads = [
+        load(light_hbm.at[:, pl.ds(t * LEAF, LEAF)], window.at[HALO + t], 4 + t) for t in range(LEAVES)
+    ]
+    basis_load = load(basis_hbm, basis, 1)
+    transfer_load = load(transfer_hbm, transfer, 2)
+    coupling_load = load(coupling_hbm, coupling, 3)
 
     geo[HALO : HALO + LEAVES] = jnp.zeros((LEAVES, 8, LEAF), F32)
     for t in range(LEAVES):
@@ -305,6 +304,12 @@
     for t in range(LEAVES // 2):
         add_tile(t, HALO + t, 0.0, 0.0, t % TILES)
 
+
+    def rejoin(height):
+        tree[height][2].wait_recv()
+        total = mine[height] + partner[height]
+        tree.append(climb(height + 1, total[:, :RANK]))
+
     arrive(0)
     to_right(0)
     arrive(2)
@@ -318,62 +323,62 @@
         to_left(n)
     for n in range(CHUNKS):
         to_sibling(chunk(n, 1))
+    rejoin(0)
     for t in range(LEAVES // 2, LEAVES):
         add_tile(t, HALO + t, 0.0, 0.0, t % TILES)
-
-    def rejoin(height):
-        tree[height][2].wait_recv()
-        total = mine[height] + partner[height]
-        tree.append(climb(height + 1, total[:, :RANK]))
-
     for move in halos:
         move.wait_recv()
 
-    def pass_step(n, carry):
+    def take(n, onward):
         ref = chunk(n + CHUNKS, 1)
         send(ref, ref, right_send, right_recv.at[n], right).wait_recv()
-        send(ref, ref, right_send, right_recv.at[n + CHUNKS], right).start()
+        if onward:
+            send(ref, ref, right_send, right_recv.at[n + CHUNKS], right).start()
         ref_left = chunk(n + CHUNKS, -1)
         send(ref_left, ref_left, left_send, left_recv.at[n], left).wait_recv()
-        send(ref_left, ref_left, left_send, left_recv.at[n + CHUNKS], left).start()
+        if onward:
+            send(ref_left, ref_left, left_send, left_recv.at[n + CHUNKS], left).start()
         to_sibling(ref)
         to_sibling(ref_left)
-        for i in range(TILES):
-            near_pair(TILES * n + i, i)
-        return carry
-
-    def last_step(n, carry):
-        ref = chunk(n + CHUNKS, 1)
-        send(ref, ref, right_send, right_recv.at[n], right).wait_recv()
-        to_sibling(ref)
-        ref_left = chunk(n + CHUNKS, -1)
-        send(ref_left, ref_left, left_send, left_recv.at[n], left).wait_recv()
-        to_sibling(ref_left)
-        return carry
-
-    done = 0
-    for height in range(UPLV):
-        lax.fori_loop(done, 3 * height + 2, pass_step, 0)
-        done = 3 * height + 2
-        rejoin(height)
-    lax.fori_loop(done, PASSED, pass_step, 0)
-    for p in range(TILES * PASSED, LEAVES * NNEAR):
-        near_pair(p, p % TILES)
-
-    downward = None
-    for height in range(UPLV, -1, -1):
+
+    def couple(height):
         tree[height][0].wait_recv()
         tree[height][1].wait_recv()
         cluster = me // 2**height
         low = jnp.where(cluster >= 2, below[height][:, :RANK], 0.0)
         high = jnp.where(cluster + 2 < devices // 2**height, above[height][:, :RANK], 0.0)
-        value = exact(low, upper_ref[height, 0]) + exact(high, upper_ref[height, 1])
-        if downward is not None:
-            value += exact(downward, up_ref[height, cluster % 2], NT)
-        downward = value
+        return exact(low, upper_ref[height, 0]) + exact(high, upper_ref[height, 1])
+
+    coupled = []
+    def ring_step(n, carry):
+        take(n, True)
+        for k in range(TILES):
+            near_pair(TILES * n + k, k)
+        return carry
+
+    for place in range(5):
+        lax.fori_loop(2 * place, 2 * place + 2, ring_step, 0)
+        if place in (0, 2):
+            rejoin(1 + place // 2)
+        if place in (1, 3):
+            coupled.append(couple(place // 2))
+    for p in range(TILES * 10, LEAVES * NNEAR):
+        near_pair(p, p % TILES)
+    coupled.append(couple(2))
+
+    def last_step(n, carry):
+        take(n, False)
+        return carry
+
+    lax.fori_loop(10, 12, last_step, 0)
+
+    coupled.append(couple(UPLV))
+    downward = coupled[UPLV]
+    for height in range(UPLV - 1, -1, -1):
+        downward = coupled[height] + exact(downward, up_ref[height, (me // 2**height) % 2], NT)
     pulled[...] = exact(downward, transfer[...], NT)
 
-    lax.fori_loop(PASSED, STEPS, last_step, 0)
+    lax.fori_loop(12, STEPS, last_step, 0)
 
     coupling_load.wait()
 
@@ -381,17 +386,16 @@
     send(others, others, sib_send, sib_recv, sibling).wait_recv()
 
     for t in range(LEAVES):
-        picked, weights = [], []
-        for c in range(NFAR):
-            code = codes[t, c]
-            picked.append(pool[code >> 1] * mask[code & 1])
-            cut = coupling[t, c * RANK : (c + 1) * RANK, :]
-            weights += [cut, cut]
-        far = jnp.dot(
-            jnp.concatenate(picked, axis=1),
-            jnp.concatenate(weights, axis=0),
-            preferred_element_type=F32,
-        )
+        picked = []
+        for c in range(0, NFAR, 2):
+            two = []
+            for k in range(2):
+                code = codes[t, c + k]
+                block = pool[code >> 1]
+                turned = jnp.concatenate([block[:, RANK:], block[:, :RANK]], axis=1)
+                two.append(jnp.where((code & 1) == k, block, turned))
+            picked.append(two[0] * mask[0] + two[1] * mask[1])
+        far = jnp.dot(jnp.concatenate(picked, axis=1), coupling[t], preferred_element_type=F32)
         leaf_far = (far + pulled[:, t * RANK : (t + 1) * RANK]).astype(BF16)
         back = jnp.dot(leaf_far, basis[t], preferred_element_type=F32)
         out_ref[:, t * LEAF : (t + 1) * LEAF] = (near_terms[t] + back).astype(BF16)
@@ -430,7 +434,7 @@
         slots = LEAVES + 2 * HALO
         return pl.pallas_call(
             functools.partial(kernel, devices),
-            out_shape=jax.ShapeDtypeStruct((LIGHTS, LEAVES * LEAF), BF16),
+            out_shape=pltpu.VMEM((LIGHTS, LEAVES * LEAF), BF16),
             in_specs=[any_space, vmem, smem, smem, any_space, any_space, any_space, vmem, vmem],
             out_specs=vmem,
             scratch_shapes=[

time: 45.3 us -> 41.8 us (0.923)
  Pallas kernels: 43.6 us -> 41 us
  local copies, waits for them, and re-layouts: 1.57 us -> 0.66 us
    pallas_call x1, Pallas kernels: 43.6 us -> 41 us  [per_device(): pl.pallas_call(functools.partial(kernel, devices), out_shape=pltpu.VMEM((...]
    unnamed x1, local copies, waits for them, and re-layouts: 1.57 us -> 0.66 us
where the time goes in v4:
time: 41.8 us; the launch traced here: 41.7 us
  Pallas kernels  41 us (98%)
  local copies, waits for them, and re-layouts  0.66 us (2%)
    pallas_call x1, Pallas kernels, per_device(): pl.pallas_call(functools.partial(kernel, devices), out_shape=pltpu.VMEM((...  41 us

profile of v4, /device:TPU:1, one launch (start us, length us, event | category | flops | bytes accessed | tf_op | source)
XLA Modules:
  0.0 41.7 jit_solution(11722458062919325602)
XLA Ops:
  0.0 41.0 %shard_map.91 = bf16[32,2048]{1,0:T(8,128)(2,1)S(1)} custom-call(bf16[32,2048]{1,0:T(8,128)(2,1)} %light_hbm.1, bf16[4,2048]{1,0:T(4,128)(2,1)} %probes_ref.1, s32[4,8]{1,0:T(4,128)} %bitcast.7, s32[8,32]{1,0:T(8,128)} %far_list_ref.1, bf16[8,64,256]{2,1,0:T(8,128)(2,1)} %bitcast.5, bf16[512,64]{1,0:T(8,128)(2,1)} %bitcast.6, bf16[8,2048,64]{2,1,0:T(8,128)(2,1)} %bitcast.4, ...), custom_call_target="tpu_custom_call" | custom-call | tf_op jit(solution)/shard_map/pallas_call | solution.py:435
  41.0 0.7 %copy.11 = bf16[32,2048]{1,0:T(8,128)(2,1)} copy(bf16[32,2048]{1,0:T(8,128)(2,1)S(1)} %shard_map.91) | data formatting | bytes 262144

commit v5 on v4

--- a/solution.py
+++ b/solution.py
@@ -25,8 +25,10 @@
 LINE = RING * RING
 PER_CHIP = 4
 CHUNKS = 4
-CHUNK = RING // CHUNKS * PER_CHIP
+PART = RING // CHUNKS
+CHUNK = PART * PER_CHIP
 STEPS = RING // 2 * CHUNKS - CHUNKS // 2
+SPLIT = CHUNKS // 4
 TILES = 3
 
 NT = (((1,), (1,)), ((), ()))
@@ -179,10 +181,10 @@
     pl.semaphore_wait(barrier, len(friends))
 
     ours, theirs = pool.at[pl.ds(my_block, 2)], pool.at[pl.ds(other_block, 2)]
-    for k in range(RING):
-        send(traded, theirs, first_send, first_recv.at[second // 2], across(first, second + k)).start()
+    for k in (0, 1, -1, 2, -2, 3, -3, 4):
+        send(traded, theirs, first_send, first_recv.at[second // PART], across(first, second + k)).start()
         if k:
-            send(ours, ours, first_send, first_recv.at[first // 2], chip(first + k, second)).start()
+            send(ours, ours, first_send, first_recv.at[first // PART], chip(first + k, second)).start()
     halos = halo(geo, 0) + halo(window, 2)
 
     transfer_load.wait()
@@ -238,13 +240,17 @@
 
     tree = [climb(0, level0)]
 
+    def place_of(n, sign):
+        p = lax.rem(n + (CHUNKS // 2) * (sign < 0), CHUNKS)
+        return lax.rem(2 * p, CHUNKS) + p // (CHUNKS // 2)
+
     def chunk(n, sign):
         b = lax.rem(second - sign * (n // CHUNKS) + RING, RING)
-        q = lax.rem(first // 2 + n + (CHUNKS // 2) * (sign < 0) + 2 * RING, CHUNKS)
+        q = lax.rem(first // PART + place_of(n, sign), CHUNKS)
         return pool.at[pl.ds((core * LINE + b * RING) * PER_CHIP + q * CHUNK, CHUNK)]
 
     def arrive(q):
-        at = lax.rem(first // 2 + q, CHUNKS)
+        at = lax.rem(first // PART + q, CHUNKS)
         ref = pool.at[pl.ds(0, CHUNK if q else CHUNK - 2)]
         send(ref, ref, first_send, first_recv.at[at], sibling).wait_recv()
 
@@ -300,7 +306,6 @@
 
     for t in range(LEAVES):
         spread_columns(t)
-    lax.fori_loop(0, LEAVES, encode, 0)
     for t in range(LEAVES // 2):
         add_tile(t, HALO + t, 0.0, 0.0, t % TILES)
 
@@ -310,20 +315,18 @@
         total = mine[height] + partner[height]
         tree.append(climb(height + 1, total[:, :RANK]))
 
-    arrive(0)
-    to_right(0)
-    arrive(2)
-    to_left(0)
-    arrive(1)
-    to_right(1)
-    arrive(3)
-    to_left(1)
-    for n in (2, 3):
+    for n in range(CHUNKS // 2):
+        arrive(2 * n)
+        to_right(n)
+        arrive(2 * n + 1)
+        to_left(n)
+    for n in range(CHUNKS // 2, CHUNKS):
         to_right(n)
         to_left(n)
-    for n in range(CHUNKS):
-        to_sibling(chunk(n, 1))
+    line = pool.at[pl.ds((core * LINE + second * RING) * PER_CHIP, RING * PER_CHIP)]
+    to_sibling(line)
     rejoin(0)
+    lax.fori_loop(0, LEAVES, encode, 0)
     for t in range(LEAVES // 2, LEAVES):
         add_tile(t, HALO + t, 0.0, 0.0, t % TILES)
     for move in halos:
@@ -351,13 +354,15 @@
 
     coupled = []
     def ring_step(n, carry):
-        take(n, True)
+        for k in range(SPLIT):
+            take(SPLIT * n + k, True)
         for k in range(TILES):
             near_pair(TILES * n + k, k)
         return carry
 
     for place in range(5):
-        lax.fori_loop(2 * place, 2 * place + 2, ring_step, 0)
+        for n in (2 * place, 2 * place + 1):
+            ring_step(n, 0)
         if place in (0, 2):
             rejoin(1 + place // 2)
         if place in (1, 3):
@@ -370,7 +375,8 @@
         take(n, False)
         return carry
 
-    lax.fori_loop(10, 12, last_step, 0)
+    for n in range(10 * SPLIT, 12 * SPLIT):
+        last_step(n, 0)
 
     coupled.append(couple(UPLV))
     downward = coupled[UPLV]
@@ -378,9 +384,21 @@
         downward = coupled[height] + exact(downward, up_ref[height, (me // 2**height) % 2], NT)
     pulled[...] = exact(downward, transfer[...], NT)
 
-    lax.fori_loop(12, STEPS, last_step, 0)
+    for n in range(12 * SPLIT, STEPS):
+        last_step(n, 0)
 
     coupling_load.wait()
+
+    for move in halos + [m for moves in tree for m in moves]:
+        move.wait_send()
+
+    def sent(count, send_sem):
+        ref = pool.at[pl.ds(0, count)]
+        send(ref, ref, send_sem, sib_recv, sibling).wait_send()
+
+    sent(2 * (2 * RING - 1), first_send)
+    sent(STEPS * CHUNK, right_send)
+    sent(STEPS * CHUNK, left_send)
 
     others = pool.at[pl.ds((1 - core) * LINE * PER_CHIP, LINE * PER_CHIP)]
     send(others, others, sib_send, sib_recv, sibling).wait_recv()
@@ -400,16 +418,6 @@
         back = jnp.dot(leaf_far, basis[t], preferred_element_type=F32)
         out_ref[:, t * LEAF : (t + 1) * LEAF] = (near_terms[t] + back).astype(BF16)
 
-    for move in halos + [m for moves in tree for m in moves]:
-        move.wait_send()
-
-    def sent(count, send_sem):
-        ref = pool.at[pl.ds(0, count)]
-        send(ref, ref, send_sem, sib_recv, sibling).wait_send()
-
-    sent(2 * (2 * RING - 1), first_send)
-    sent(STEPS * CHUNK, right_send)
-    sent(STEPS * CHUNK, left_send)
     sent(LINE * PER_CHIP, sib_send)
 
 

time: 41.8 us -> 41.5 us (level)
  no operation moved by 1% of the time
where the time goes in v5:
time: 41.5 us; the launch traced here: 41.4 us
  Pallas kernels  40.7 us (98%)
  local copies, waits for them, and re-layouts  0.66 us (2%)
    pallas_call x1, Pallas kernels, per_device(): pl.pallas_call(functools.partial(kernel, devices), out_shape=pltpu.VMEM((...  40.7 us

profile of v5, /device:TPU:1, one launch (start us, length us, event | category | flops | bytes accessed | tf_op | source)
XLA Modules:
  0.0 41.4 jit_solution(5156752632593750811)
XLA Ops:
  0.0 40.7 %shard_map.91 = bf16[32,2048]{1,0:T(8,128)(2,1)S(1)} custom-call(bf16[32,2048]{1,0:T(8,128)(2,1)} %light_hbm.1, bf16[4,2048]{1,0:T(4,128)(2,1)} %probes_ref.1, s32[4,8]{1,0:T(4,128)} %bitcast.7, s32[8,32]{1,0:T(8,128)} %far_list_ref.1, bf16[8,64,256]{2,1,0:T(8,128)(2,1)} %bitcast.5, bf16[512,64]{1,0:T(8,128)(2,1)} %bitcast.6, bf16[8,2048,64]{2,1,0:T(8,128)(2,1)} %bitcast.4, ...), custom_call_target="tpu_custom_call" | custom-call | tf_op jit(solution)/shard_map/pallas_call | solution.py:443
  40.7 0.7 %copy.11 = bf16[32,2048]{1,0:T(8,128)(2,1)} copy(bf16[32,2048]{1,0:T(8,128)(2,1)S(1)} %shard_map.91) | data formatting | bytes 262144

commit v6 on v5

--- a/solution.py
+++ b/solution.py
@@ -37,15 +37,20 @@
 def kernel(
     devices,
     light_hbm,
-    probes_ref,
-    near_list_ref,
-    far_list_ref,
+    probes_hbm,
+    near_list_hbm,
+    far_list_hbm,
     basis_hbm,
     transfer_hbm,
     coupling_hbm,
+    up_hbm,
+    upper_hbm,
+    out_ref,
+    near_list_ref,
+    far_list_ref,
+    probes_ref,
     up_ref,
     upper_ref,
-    out_ref,
     window,
     geo,
     columns,
@@ -118,13 +123,19 @@
         copy.start()
         return copy
 
+    probes_load = load(probes_hbm, probes_ref, 0)
     light_loads = [
         load(light_hbm.at[:, pl.ds(t * LEAF, LEAF)], window.at[HALO + t], 4 + t) for t in range(LEAVES)
     ]
     basis_load = load(basis_hbm, basis, 1)
     transfer_load = load(transfer_hbm, transfer, 2)
     coupling_load = load(coupling_hbm, coupling, 3)
-
+    near_load = load(near_list_hbm, near_list_ref, 6 + LEAVES)
+    far_load = load(far_list_hbm, far_list_ref, 7 + LEAVES)
+    up_load = load(up_hbm, up_ref, 4 + LEAVES)
+    upper_load = load(upper_hbm, upper_ref, 5 + LEAVES)
+
+    probes_load.wait()
     geo[HALO : HALO + LEAVES] = jnp.zeros((LEAVES, 8, LEAF), F32)
     for t in range(LEAVES):
         geo[HALO + t, 0:4, :] = probes_ref[:, t * LEAF : (t + 1) * LEAF].astype(F32)
@@ -188,6 +199,10 @@
     halos = halo(geo, 0) + halo(window, 2)
 
     transfer_load.wait()
+    near_load.wait()
+    far_load.wait()
+    up_load.wait()
+    upper_load.wait()
     stacked = jnp.concatenate(pairs, axis=1)
     level0 = jnp.dot(stacked, transfer[...], preferred_element_type=F32)
 
@@ -437,15 +452,19 @@
     ):
         any_space = pl.BlockSpec(memory_space=pl.ANY)
         vmem = pl.BlockSpec(memory_space=pltpu.VMEM)
-        smem = pl.BlockSpec(memory_space=pltpu.SMEM)
         dma = pltpu.SemaphoreType.DMA
         slots = LEAVES + 2 * HALO
         return pl.pallas_call(
             functools.partial(kernel, devices),
             out_shape=pltpu.VMEM((LIGHTS, LEAVES * LEAF), BF16),
-            in_specs=[any_space, vmem, smem, smem, any_space, any_space, any_space, vmem, vmem],
+            in_specs=[any_space] * 9,
             out_specs=vmem,
             scratch_shapes=[
+                pltpu.SMEM((NNEAR, LEAVES), jnp.int32),
+                pltpu.SMEM((LEAVES, NFAR), jnp.int32),
+                pltpu.VMEM((4, LEAVES * LEAF), BF16),
+                pltpu.VMEM(up_transfer.shape, BF16),
+                pltpu.VMEM(upper_coupling.shape, BF16),
                 pltpu.VMEM((slots, LIGHTS, LEAF), BF16),
                 pltpu.VMEM((slots, 8, LEAF), F32),
                 pltpu.VMEM((LEAVES, 4, LEAF, 128), F32),
@@ -464,7 +483,7 @@
                 pltpu.VMEM((UPLV + 1, LIGHTS, 2 * RANK), F32),
                 pltpu.VMEM((2, LIGHTS, 2 * RANK), BF16),
                 pltpu.SMEM((LEAVES, NFAR), jnp.int32),
-                dma((4 + LEAVES,)),
+                dma((8 + LEAVES,)),
                 dma((4,)),
                 dma((4,)),
                 dma,

time: 41.5 us -> 40.6 us (0.978)
  Pallas kernels: 40.7 us -> 39.8 us
    pallas_call x1, Pallas kernels: 40.7 us -> 39.8 us  [per_device(): pl.pallas_call(functools.partial(kernel, devices), out_shape=pltpu.VMEM((...]
where the time goes in v6:
time: 40.6 us; the launch traced here: 40.4 us
  Pallas kernels  39.8 us (98%)
  local copies, waits for them, and re-layouts  0.66 us (2%)
    pallas_call x1, Pallas kernels, per_device(): pl.pallas_call(functools.partial(kernel, devices), out_shape=pltpu.VMEM((...  39.8 us

profile of v6, /device:TPU:1, one launch (start us, length us, event | category | flops | bytes accessed | tf_op | source)
XLA Modules:
  0.0 40.4 jit_solution(5019162431731517877)
XLA Ops:
  0.0 39.8 %shard_map.91 = bf16[32,2048]{1,0:T(8,128)(2,1)S(1)} custom-call(bf16[32,2048]{1,0:T(8,128)(2,1)} %light_hbm.1, bf16[4,2048]{1,0:T(4,128)(2,1)} %probes_hbm.1, s32[4,8]{1,0:T(4,128)} %bitcast.7, s32[8,32]{1,0:T(8,128)} %far_list_hbm.1, bf16[8,64,256]{2,1,0:T(8,128)(2,1)} %bitcast.5, bf16[512,64]{1,0:T(8,128)(2,1)} %bitcast.6, bf16[8,2048,64]{2,1,0:T(8,128)(2,1)} %bitcast.4, ...), custom_call_target="tpu_custom_call" | custom-call | tf_op jit(solution)/shard_map/pallas_call | solution.py:457
  39.8 0.7 %copy.11 = bf16[32,2048]{1,0:T(8,128)(2,1)} copy(bf16[32,2048]{1,0:T(8,128)(2,1)S(1)} %shard_map.91) | data formatting | bytes 262144

commit v7 on v6

--- a/solution.py
+++ b/solution.py
@@ -321,9 +321,6 @@
 
     for t in range(LEAVES):
         spread_columns(t)
-    for t in range(LEAVES // 2):
-        add_tile(t, HALO + t, 0.0, 0.0, t % TILES)
-
 
     def rejoin(height):
         tree[height][2].wait_recv()
@@ -342,7 +339,7 @@
     to_sibling(line)
     rejoin(0)
     lax.fori_loop(0, LEAVES, encode, 0)
-    for t in range(LEAVES // 2, LEAVES):
+    for t in range(LEAVES):
         add_tile(t, HALO + t, 0.0, 0.0, t % TILES)
     for move in halos:
         move.wait_recv()

time: 40.6 us -> 41 us (level)
  no operation moved by 1% of the time
where the time goes in v7:
time: 41 us; the launch traced here: 40.8 us
  Pallas kernels  40.2 us (98%)
  local copies, waits for them, and re-layouts  0.66 us (2%)
    pallas_call x1, Pallas kernels, per_device(): pl.pallas_call(functools.partial(kernel, devices), out_shape=pltpu.VMEM((...  40.2 us

profile of v7, /device:TPU:1, one launch (start us, length us, event | category | flops | bytes accessed | tf_op | source)
XLA Modules:
  0.0 40.8 jit_solution(8690110328302747657)
XLA Ops:
  0.0 40.2 %shard_map.91 = bf16[32,2048]{1,0:T(8,128)(2,1)S(1)} custom-call(bf16[32,2048]{1,0:T(8,128)(2,1)} %light_hbm.1, bf16[4,2048]{1,0:T(4,128)(2,1)} %probes_hbm.1, s32[4,8]{1,0:T(4,128)} %bitcast.7, s32[8,32]{1,0:T(8,128)} %far_list_hbm.1, bf16[8,64,256]{2,1,0:T(8,128)(2,1)} %bitcast.5, bf16[512,64]{1,0:T(8,128)(2,1)} %bitcast.6, bf16[8,2048,64]{2,1,0:T(8,128)(2,1)} %bitcast.4, ...), custom_call_target="tpu_custom_call" | custom-call | tf_op jit(solution)/shard_map/pallas_call | solution.py:454
  40.2 0.7 %copy.11 = bf16[32,2048]{1,0:T(8,128)(2,1)} copy(bf16[32,2048]{1,0:T(8,128)(2,1)S(1)} %shard_map.91) | data formatting | bytes 262144
